TPU v7x, 32 devices: a whole 2x2x4 slice. The times are simulated.
32 devices in a mesh: tm: 8 (over z, x), height: 2 (over y), dp: 2 (over core).
Axes of the slice: x: 2, y: 2, z: 4, core: 2. Of those that a mesh axis runs over, the one named last changes fastest.
Arguments:
- frames_in: bfloat16 [2, 32, 8, 48, 256], P('dp', 'tm', 'height'), may hold values from -6 to 6
- cotangent: bfloat16 [2, 32, 8, 48, 256], P('dp', 'tm', 'height'), may hold values from -6 to 6
- w_spatial: bfloat16 [3, 3, 256, 256], replicated, may hold values from -0.125 to 0.125
- w_temporal: bfloat16 [3, 256, 256], replicated, may hold values from -0.21875 to 0.21875
Outputs:
- decoded: bfloat16 [2, 32, 8, 48, 256], P('dp', 'tm', 'height')
- input_grad: bfloat16 [2, 32, 8, 48, 256], P('dp', 'tm', 'height')
- spatial_grad: bfloat16 [3, 3, 256, 256], replicated
- temporal_grad: bfloat16 [3, 256, 256], replicated
All inputs are finite; a program needn't handle non-finite values.
Results may differ from a plain program's by a relative error of at most 0.0061.
Values may be sent and summed in bfloat16 or wider, within the bound.
A program may use at most 64 MiB of HBM per device.

v0:
```python
import math

import jax
import jax.numpy as jnp
from jax import lax
from jax.sharding import PartitionSpec as P


def extended(x, sides, width):
    for axis, dim in sides:
        count, length = (lax.axis_size(axis), x.shape[dim])
        up = [(i, (i + 1) % count) for i in range(count - 1)]
        down = [(j, i) for i, j in up]
        last = lax.slice_in_dim(x, length - width, length, axis=dim)
        initial = lax.slice_in_dim(x, 0, width, axis=dim)
        before = lax.ppermute(last, axis, up)
        after = lax.ppermute(initial, axis, down)
        x = jnp.concatenate([before, x, after], axis=dim)
    return x


def from_behind(block, axis, distance):
    devices = range(lax.axis_size(axis))
    route = [(i - distance, i) for i in devices if i - distance in devices]
    return lax.ppermute(block, axis, route)


def silu_slope(values):
    sigmoid_value = jax.nn.sigmoid(values)
    return sigmoid_value * (1.0 + values * (1.0 - sigmoid_value))


def forward_taps(padded, row_count, col_count):
    pieces = [
        padded[:, row_tap : row_tap + row_count, col_tap : col_tap + col_count]
        for row_tap in range(3)
        for col_tap in range(3)
    ]
    return jnp.concatenate(pieces, axis=-1)


def backward_taps(padded, row_count, col_count):
    pieces = [
        padded[:, 2 - row_tap : 2 - row_tap + row_count, 2 - col_tap : 2 - col_tap + col_count]
        for row_tap in range(3)
        for col_tap in range(3)
    ]
    return jnp.concatenate(pieces, axis=-1)


def frame_taps(source, frame_count):
    return jnp.concatenate(
        [source[shift_tap : shift_tap + frame_count] for shift_tap in range(3)], axis=-1
    )


def flat_dot(left_side, right_side):
    return jnp.dot(
        left_side.reshape(-1, left_side.shape[-1]), right_side, preferred_element_type=jnp.float32
    )


def local(frames_in, cotangent, w_spatial, w_temporal):
    inputs = frames_in[0]
    upstream = cotangent[0]
    frame_count, row_count, col_count, channels = inputs.shape
    spatial_flat = w_spatial.reshape(9 * channels, channels)
    temporal_flat = w_temporal.reshape(3 * channels, channels)
    spatial_back = jnp.concatenate(
        [w_spatial[row_tap, col_tap].T for row_tap in range(3) for col_tap in range(3)], axis=0
    )
    temporal_back = jnp.concatenate([w_temporal[2].T, w_temporal[1].T, w_temporal[0].T], axis=0)
    first_shard = lax.axis_index("tm") == 0
    activated = jax.nn.silu(inputs.astype(jnp.float32)).astype(jnp.bfloat16)
    activ_rows = extended(activated, (("height", 1),), 1)
    activ_pad = jnp.pad(activ_rows, ((0, 0), (0, 0), (1, 1), (0, 0)))
    activ_taps = forward_taps(activ_pad, row_count, col_count).reshape(-1, 9 * channels)
    spatial_out = jnp.dot(activ_taps, spatial_flat, preferred_element_type=jnp.float32)
    spatial_out = spatial_out.astype(jnp.bfloat16).reshape(inputs.shape)
    earlier = from_behind(spatial_out[frame_count - 2 :], "tm", 1)
    repeated = jnp.broadcast_to(spatial_out[:1], earlier.shape)
    earlier = jnp.where(first_shard, repeated, earlier)
    padded_frames = jnp.concatenate([earlier, spatial_out], axis=0)
    frame_stack = frame_taps(padded_frames, frame_count).reshape(-1, 3 * channels)
    temporal_out = jnp.dot(frame_stack, temporal_flat, preferred_element_type=jnp.float32).reshape(
        inputs.shape
    )
    decoded = (inputs.astype(jnp.float32) + temporal_out).astype(jnp.bfloat16)
    upstream_ext = jnp.pad(upstream, ((2, 2), (0, 0), (0, 0), (0, 0)))
    frame_part = flat_dot(frame_taps(upstream_ext, frame_count + 2), temporal_back)
    frame_part = frame_part.reshape(frame_count + 2, row_count, col_count, channels)
    rim_part = frame_part[:2]
    returned = from_behind(rim_part, "tm", -1)
    frame_sum = frame_part[2:]
    frame_sum = frame_sum.at[frame_count - 2 :].add(returned)
    frame_sum = frame_sum.at[0].add(jnp.where(first_shard, rim_part[0] + rim_part[1], 0.0))
    frame_grad = frame_sum.astype(jnp.bfloat16)
    grad_pad = jnp.pad(frame_grad, ((0, 0), (2, 2), (1, 1), (0, 0)))
    grad_ext = flat_dot(backward_taps(grad_pad, row_count + 2, col_count), spatial_back)
    grad_ext = grad_ext.reshape(frame_count, row_count + 2, col_count, channels)
    edge_rows = jnp.stack([grad_ext[:, 0], grad_ext[:, row_count + 1]], axis=1)
    arrived = extended(edge_rows.astype(jnp.bfloat16), (("height", 1),), 1).astype(edge_rows.dtype)
    act_grad = grad_ext[:, 1 : row_count + 1]
    act_grad = act_grad.at[:, 0].add(arrived[:, 0])
    act_grad = act_grad.at[:, row_count - 1].add(arrived[:, 3])
    input_grad = (
        upstream.astype(jnp.float32) + silu_slope(inputs.astype(jnp.float32)) * act_grad
    ).astype(jnp.bfloat16)
    cell_count = (
        frame_count
        * lax.axis_size("tm")
        * row_count
        * lax.axis_size("height")
        * col_count
        * lax.axis_size("dp")
    )
    grad_scale = 1.0 / math.sqrt(cell_count)
    contract = (((0,), (0,)), ((), ()))
    spatial_term = lax.dot_general(
        activ_taps, frame_grad.reshape(-1, channels), contract, preferred_element_type=jnp.float32
    )
    temporal_term = lax.dot_general(
        frame_stack, upstream.reshape(-1, channels), contract, preferred_element_type=jnp.float32
    )
    weight_terms = jnp.concatenate([spatial_term, temporal_term], axis=0) * grad_scale
    summed = lax.psum(weight_terms, ("tm", "height", "dp")).astype(jnp.bfloat16)
    spatial_grad = summed[: 9 * channels].reshape(3, 3, channels, channels)
    temporal_grad = summed[9 * channels :].reshape(3, channels, channels)
    return (decoded[None], input_grad[None], spatial_grad, temporal_grad)


def solution(mesh):
    return jax.shard_map(
        local,
        mesh=mesh,
        in_specs=(
            P("dp", "tm", "height", None, None),
            P("dp", "tm", "height", None, None),
            P(),
            P(),
        ),
        out_specs=(
            P("dp", "tm", "height", None, None),
            P("dp", "tm", "height", None, None),
            P(),
            P(),
        ),
        check_vma=False,
    )
```

profile of v0, /device:TPU:1, one launch (start us, length us, event | category | flops | bytes accessed | tf_op | source)
XLA Modules:
  0.0 141.6 jit_solution(13488378569690186072)
XLA Ops:
  0.6 1.5 %pad_slice_fusion.11 = (bf16[6,4,48,256]{3,2,1,0:T(8,128)(2,1)S(1)}, bf16[6,4,48,256]{3,2,1,0:T(8,128)(2,1)S(1)}, bf16[6,4,48,256]{3,2,1,0:T(8,128)(2,1)S(1)}) fusion(bf16[4,4,48,256]{3,2,1,0:T(8,128)(2,1)} %bitcast.104), kind=kLoop, calls=%fused_computation.37 | loop fusion | bytes 2162688 | tf_op jit(solution)/shard_map/slice | solution.py:53
  3.8 1.3 collective-permute-start.3
  5.2 1.0 fusion.56
  6.2 1.0 copy.20
  8.9 1.0 copy.22
  12.0 1.0 copy.25
  14.0 1.0 copy.27
  20.5 1.0 add_dynamic-update-slice_fusion
  23.3 1.6 %fusion.60 = (bf16[4,6,48,256]{3,2,1,0:T(8,128)(2,1)S(1)}, f32[4,6,48,256]{3,2,1,0:T(8,128)S(1)}) fusion(bf16[4,6,48,2304]{3,2,1,0:T(8,128)(2,1)S(1)} %fusion.38, bf16[2304,256]{1,0:T(8,128)(2,1)S(1)} %copy-done.13), kind=kOutput, calls=%fused_computation.115 | convolution fusion | flops 1359249408 | bytes 8257536 | tf_op jit(solution)/shard_map/dot_general | solution.py:58
  25.0 4.1 %collective-permute-start.4 = (bf16[4,1,48,256]{3,2,1,0:T(8,128)(2,1)S(1)}, bf16[4,1,48,256]{3,2,1,0:T(8,128)(2,1)S(1)}, u32[]{:S(2)}, u32[]{:S(2)}) collective-permute-start(bf16[4,1,48,256]{3,2,1,0:T(8,128)(2,1)S(1)} %get-tuple-element.63), channel_id=1, source_target_pairs={{0,2},{1,3},{4,6},{5,7},{8,10},{9,11},{12,14},{13,15},{16,18},{17,... | collective-permute-start | bytes 294920 | tf_op jit(solution)/shard_map/ppermute | solution.py:16
  29.1 1.3 collective-permute-start.5
  30.7 3.7 %collective-permute-done.5 = bf16[4,1,48,256]{3,2,1,0:T(8,128)(2,1)S(1)} collective-permute-done((bf16[4,1,48,256]{3,2,1,0:T(8,128)(2,1)S(1)}, bf16[4,1,48,256]{3,2,1,0:T(8,128)(2,1)S(1)}, u32[]{:S(2)}, u32[]{:S(2)}) %collective-permute-start.5) | collective-permute-done | bytes 98336 | tf_op jit(solution)/shard_map/ppermute | solution.py:17
  34.5 1.1 fusion.48
  35.7 1.5 %collective-permute-start = (bf16[4,1,48,256]{3,2,1,0:T(8,128)(2,1)S(1)}, bf16[4,1,48,256]{3,2,1,0:T(8,128)(2,1)S(1)}, u32[]{:S(2)}, u32[]{:S(2)}) collective-permute-start(bf16[4,1,48,256]{3,2,1,0:T(8,128)(2,1)S(1)} %get-tuple-element.75), channel_id=1, source_target_pairs={{0,2},{1,3},{4,6},{5,7},{8,10},{9,11},{12,14},{13,15},{16,18},{17,... | collective-permute-start | bytes 294920 | tf_op jit(solution)/shard_map/ppermute | solution.py:16
  37.2 1.3 collective-permute-start.1
  38.8 3.7 %collective-permute-done.1 = bf16[4,1,48,256]{3,2,1,0:T(8,128)(2,1)S(1)} collective-permute-done((bf16[4,1,48,256]{3,2,1,0:T(8,128)(2,1)S(1)}, bf16[4,1,48,256]{3,2,1,0:T(8,128)(2,1)S(1)}, u32[]{:S(2)}, u32[]{:S(2)}) %collective-permute-start.1) | collective-permute-done | bytes 98336 | tf_op jit(solution)/shard_map/ppermute | solution.py:17
  44.4 1.1 convolution_convert_fusion
  45.5 4.0 %collective-permute-start.2 = (bf16[2,4,48,256]{3,2,1,0:T(8,128)(2,1)S(1)}, bf16[2,4,48,256]{3,2,1,0:T(8,128)(2,1)S(1)}, u32[]{:S(2)}, u32[]{:S(2)}) collective-permute-start(bf16[2,4,48,256]{3,2,1,0:T(8,128)(2,1)S(1)} %bitcast.117), channel_id=1, source_target_pairs={{0,4},{4,8},{8,12},{12,16},{16,20},{20,24},{24,28},{1,5},{5,9},{9,... | collective-permute-start | bytes 589832 | tf_op jit(solution)/shard_map/ppermute | solution.py:25
  49.5 1.2 convolution_bitcast_fusion
  50.7 1.4 collective-permute-done.2
  53.8 82.3 %all-reduce.4 = bf16[3072,256]{1,0:T(8,128)(2,1)} all-reduce(f32[3072,256]{1,0:T(8,128)S(1)} %maximum_multiply_fusion), channel_id=1, replica_groups=mesh['tm'=8,'height'=2,'dp'=2] {'tm','height','dp'}, use_global_device_ids=true, to_apply=%region_0.1 | all-reduce | flops 786432 | bytes 4718592 | tf_op jit(solution)/shard_map/psum | solution.py:126
  136.1 2.5 %slice.363 = bf16[2304,256]{1,0:T(8,128)(2,1)} slice(bf16[3072,256]{1,0:T(8,128)(2,1)} %all-reduce.4), slice={[0:2304], [0:256]} | slice | bytes 2359296 | tf_op jit(solution)/shard_map/slice | solution.py:127
  138.6 1.8 %slice.364 = bf16[768,256]{1,0:T(8,128)(2,1)} slice(bf16[3072,256]{1,0:T(8,128)(2,1)} %all-reduce.4), slice={[2304:3072], [0:256]} | slice | bytes 786432 | tf_op jit(solution)/shard_map/slice | solution.py:128
  140.4 1.2 fusion.2
  (83 shorter events, 17.7 us)
Async XLA Ops:
  0.6 1.6 %copy-start.7 = (bf16[3,256,256]{2,1,0:T(8,128)(2,1)S(1)}, bf16[3,256,256]{2,1,0:T(8,128)(2,1)}, u32[]{:S(2)}) copy-start(bf16[3,256,256]{2,1,0:T(8,128)(2,1)} %param.15) | copy-start | bytes 1179652
  3.0 2.2 %copy-start.4 = (bf16[3,3,256,256]{3,2,1,0:T(8,128)(2,1)S(1)}, bf16[3,3,256,256]{3,2,1,0:T(8,128)(2,1)}, u32[]{:S(2)}) copy-start(bf16[3,3,256,256]{3,2,1,0:T(8,128)(2,1)} %param.14) | copy-start | bytes 3538948
  3.8 16.6 %collective-permute-start.3 = (f32[2,4,48,256]{3,2,1,0:T(8,128)}, f32[2,4,48,256]{3,2,1,0:T(8,128)}, u32[]{:S(2)}, u32[]{:S(2)}) collective-permute-start(f32[2,4,48,256]{3,2,1,0:T(8,128)} %bitcast.21), channel_id=1, source_target_pairs={{4,0},{8,4},{12,8},{16,12},{20,16},{24,20},{28,24},{5,1},{9,5},{13... | collective-permute-start | bytes 1179656 | tf_op jit(solution)/shard_map/ppermute | solution.py:25
  6.2 8.8 %copy-start.6 = (bf16[1,1,256,256]{3,2,1,0:T(8,128)(2,1)S(1)}, bf16[1,1,256,256]{3,2,1,0:T(8,128)(2,1)}, u32[]{:S(2)}) copy-start(bf16[1,1,256,256]{3,2,1,0:T(8,128)(2,1)} %get-tuple-element.52) | copy-start | bytes 393220
  22.1 1.3 copy-start.13
  24.9 9.6 %copy-start = (bf16[1,4,4,48,256]{4,3,2,1,0:T(8,128)(2,1)S(1)}, bf16[1,4,4,48,256]{4,3,2,1,0:T(8,128)(2,1)}, u32[]{:S(2)}) copy-start(bf16[1,4,4,48,256]{4,3,2,1,0:T(8,128)(2,1)} %param.12) | copy-start | bytes 1179652
  24.9 9.6 %copy-start.1 = (bf16[1,4,4,48,256]{4,3,2,1,0:T(8,128)(2,1)S(1)}, bf16[1,4,4,48,256]{4,3,2,1,0:T(8,128)(2,1)}, u32[]{:S(2)}) copy-start(bf16[1,4,4,48,256]{4,3,2,1,0:T(8,128)(2,1)} %param.13) | copy-start | bytes 1179652
  25.0 5.7 %collective-permute-start.4 = (bf16[4,1,48,256]{3,2,1,0:T(8,128)(2,1)S(1)}, bf16[4,1,48,256]{3,2,1,0:T(8,128)(2,1)S(1)}, u32[]{:S(2)}, u32[]{:S(2)}) collective-permute-start(bf16[4,1,48,256]{3,2,1,0:T(8,128)(2,1)S(1)} %get-tuple-element.63), channel_id=1, source_target_pairs={{0,2},{1,3},{4,6},{5,7},{8,10},{9,11},{12,14},{13,15},{16,18},{17,... | collective-permute-start | bytes 294920 | tf_op jit(solution)/shard_map/ppermute | solution.py:16
  29.1 5.4 %collective-permute-start.5 = (bf16[4,1,48,256]{3,2,1,0:T(8,128)(2,1)S(1)}, bf16[4,1,48,256]{3,2,1,0:T(8,128)(2,1)S(1)}, u32[]{:S(2)}, u32[]{:S(2)}) collective-permute-start(bf16[4,1,48,256]{3,2,1,0:T(8,128)(2,1)S(1)} %get-tuple-element.64), channel_id=1, source_target_pairs={{2,0},{3,1},{6,4},{7,5},{10,8},{11,9},{14,12},{15,13},{18,16},{19,... | collective-permute-start | bytes 294920 | tf_op jit(solution)/shard_map/ppermute | solution.py:17
  35.7 3.2 %collective-permute-start = (bf16[4,1,48,256]{3,2,1,0:T(8,128)(2,1)S(1)}, bf16[4,1,48,256]{3,2,1,0:T(8,128)(2,1)S(1)}, u32[]{:S(2)}, u32[]{:S(2)}) collective-permute-start(bf16[4,1,48,256]{3,2,1,0:T(8,128)(2,1)S(1)} %get-tuple-element.75), channel_id=1, source_target_pairs={{0,2},{1,3},{4,6},{5,7},{8,10},{9,11},{12,14},{13,15},{16,18},{17,... | collective-permute-start | bytes 294920 | tf_op jit(solution)/shard_map/ppermute | solution.py:16
  37.2 5.4 %collective-permute-start.1 = (bf16[4,1,48,256]{3,2,1,0:T(8,128)(2,1)S(1)}, bf16[4,1,48,256]{3,2,1,0:T(8,128)(2,1)S(1)}, u32[]{:S(2)}, u32[]{:S(2)}) collective-permute-start(bf16[4,1,48,256]{3,2,1,0:T(8,128)(2,1)S(1)} %get-tuple-element.76), channel_id=1, source_target_pairs={{2,0},{3,1},{6,4},{7,5},{10,8},{11,9},{14,12},{15,13},{18,16},{19,... | collective-permute-start | bytes 294920 | tf_op jit(solution)/shard_map/ppermute | solution.py:17
  43.1 1.3 copy-start.5
  45.5 6.7 %copy-start.2 = (bf16[768,256]{1,0:T(8,128)(2,1)}, bf16[768,256]{1,0:T(8,128)(2,1)S(1)}, u32[]{:S(2)}) copy-start(bf16[768,256]{1,0:T(8,128)(2,1)S(1)} %convolution_convert_fusion) | copy-start | bytes 1179652
  45.5 6.6 %collective-permute-start.2 = (bf16[2,4,48,256]{3,2,1,0:T(8,128)(2,1)S(1)}, bf16[2,4,48,256]{3,2,1,0:T(8,128)(2,1)S(1)}, u32[]{:S(2)}, u32[]{:S(2)}) collective-permute-start(bf16[2,4,48,256]{3,2,1,0:T(8,128)(2,1)S(1)} %bitcast.117), channel_id=1, source_target_pairs={{0,4},{4,8},{8,12},{12,16},{16,20},{20,24},{24,28},{1,5},{5,9},{9,... | collective-permute-start | bytes 589832 | tf_op jit(solution)/shard_map/ppermute | solution.py:25
  52.2 0.7 copy-start.9
  52.2 0.9 copy-start.11
  136.1 4.3 %copy-start.3 = (bf16[768,256]{1,0:T(8,128)(2,1)S(1)}, bf16[768,256]{1,0:T(8,128)(2,1)}, u32[]{:S(2)}) copy-start(bf16[768,256]{1,0:T(8,128)(2,1)} %copy-done.2) | copy-start | bytes 1179652
  136.1 4.3 %copy-start.8 = (bf16[3,256,256]{2,1,0:T(8,128)(2,1)S(1)}, bf16[3,256,256]{2,1,0:T(8,128)(2,1)}, u32[]{:S(2)}) copy-start(bf16[3,256,256]{2,1,0:T(8,128)(2,1)} %param.15) | copy-start | bytes 1179652
  136.1 4.3 %copy-start.10 = (bf16[4,4,48,256]{3,2,1,0:T(8,128)(2,1)S(1)}, bf16[4,4,48,256]{3,2,1,0:T(8,128)(2,1)}, u32[]{:S(2)}) copy-start(bf16[4,4,48,256]{3,2,1,0:T(8,128)(2,1)} %copy-done.9) | copy-start | bytes 1179652
  136.1 4.3 %copy-start.12 = (bf16[4,4,48,256]{3,2,1,0:T(8,128)(2,1)S(1)}, bf16[4,4,48,256]{3,2,1,0:T(8,128)(2,1)}, u32[]{:S(2)}) copy-start(bf16[4,4,48,256]{3,2,1,0:T(8,128)(2,1)} %copy-done.11) | copy-start | bytes 1179652
where the time goes:
time: 143 us; the launch traced here: 142 us
  blocking collectives  82.3 us (58%)
  local copies, waits for them, and re-layouts  25.6 us (18%)
  starting transfers between devices  13.5 us (9%)
  waiting for transfers between devices  9.45 us (7%)
  matrix products  6.2 us (4%)
  other arithmetic  3.42 us (2%)
    psum x1, blocking collectives, local(): summed = lax.psum(weight_terms, ('tm', 'height', 'dp')).astype(jnp.bfloat16)  82.3 us
    unnamed x58, local copies, waits for them, and re-layouts  16.9 us
    ppermute x2, waiting for transfers between devices, extended(): after = lax.ppermute(initial, axis, down)  7.49 us
    ppermute x2, starting transfers between devices, extended(): before = lax.ppermute(last, axis, up)  5.65 us
    ppermute x2, starting transfers between devices, from_behind(): return lax.ppermute(block, axis, route)  5.28 us
  transfers between devices with their start and end apart: 6, of which 5 were waited for; matrix products, arithmetic and copies ran while one was open for 12% of the time, Pallas kernels for 0%

commit v1 on v0

v1 whole, which is shorter than its diff:
```python
import functools
import math

import jax
import jax.numpy as jnp
from jax import lax
from jax.experimental import pallas as pl
from jax.experimental.pallas import tpu as pltpu
from jax.sharding import PartitionSpec as P

F32 = jnp.float32
BF16 = jnp.bfloat16
GROUPS = 3


def split_bit(axis, distance):
    index = lax.axis_index(axis)
    bit = lax.rem(lax.div(index, distance), 2)
    return bit, index + distance - 2 * distance * bit


def plans(sizes):
    near = [("tm", 1), ("height", 1), ("tm", 2)]
    rest = [
        (axis, 1 << b)
        for axis in ("tm", "height")
        for b in range(sizes[axis].bit_length() - 1)
        if (axis, 1 << b) not in near
    ]
    result = []
    for g in range(GROUPS):
        order = [("dp", 1)] + near[g:] + near[:g]
        result.append([(a, d, True) for a, d in order] + [(a, d, False) for a, d in rest])
    return result


def sums_layout(plan, rows):
    spots, at, size = [], 0, rows
    for _, _, halves in plan:
        size = size // 2 if halves else size
        spots.append((at, size))
        at += size
    return spots, at


def sigmoid(v):
    return 1.0 / (1.0 + jnp.exp(-v))


def shifted(v, cols):
    cells, ch = v.shape
    col = lax.broadcasted_iota(jnp.int32, (cells // cols, cols, ch), 1).reshape(cells, ch)
    before = jnp.where(col == 0, 0.0, pltpu.roll(v, 1, 0))
    after = jnp.where(col == cols - 1, 0.0, pltpu.roll(v, cells - 1, 0))
    return before, after


def dot_nn(a, b):
    return jnp.dot(a, b, preferred_element_type=F32)


def dot_nt(a, b):
    return lax.dot_general(a, b, (((1,), (1,)), ((), ())), preferred_element_type=F32)


def dot_tn(a, b):
    return lax.dot_general(a, b, (((0,), (0,)), ((), ())), preferred_element_type=F32)


def kernel(
    sizes, scale,
    x_ref, c_ref, ws_ref, wt_ref,
    dec_ref, ig_ref, sg_ref, tg_ref,
    xh, ch, soh, fgh, so, fg, s_buf, t_buf, acc, sb, rb, full,
    halo_send, halo_recv, sum_send, sum_recv,
):
    frames, rows, cols, chan = x_ref.shape
    cells = frames * rows * cols
    tm, height = lax.axis_index("tm"), lax.axis_index("height")
    n_tm, n_h = sizes["tm"], sizes["height"]
    group_plans = plans(sizes)
    group_rows = 12 * chan // GROUPS
    spots, _ = sums_layout(group_plans[0], group_rows)

    has_prev, has_next = tm > 0, tm < n_tm - 1
    has_up, has_down = height > 0, height < n_h - 1

    barrier = pltpu.get_barrier_semaphore()

    def greet(device):
        pl.semaphore_signal(barrier, inc=1, device_id=device, device_id_type=pl.DeviceIdType.MESH)

    bits = sorted({(a, d) for a, d, _ in group_plans[0]})
    for axis, distance in bits:
        greet({axis: split_bit(axis, distance)[1]})
    pl.when(has_prev)(lambda: greet({"tm": tm - 1}))
    pl.when(has_next)(lambda: greet({"tm": tm + 1}))
    pl.when(has_up)(lambda: greet({"height": height - 1}))
    pl.when(has_down)(lambda: greet({"height": height + 1}))
    expected = len(bits) + sum(
        jnp.where(has, 1, 0) for has in (has_prev, has_next, has_up, has_down)
    )
    pl.semaphore_wait(barrier, expected)

    def remote(src, dst, sems, device):
        return pltpu.make_async_remote_copy(
            src_ref=src, dst_ref=dst, send_sem=sems[0], recv_sem=sems[1],
            device_id=device, device_id_type=pl.DeviceIdType.MESH,
        )

    def halo(at):
        return halo_send.at[at], halo_recv.at[at]

    x_up = remote(x_ref.at[:, 0], xh.at[1], halo(0), {"height": height - 1})
    x_down = remote(x_ref.at[:, rows - 1], xh.at[0], halo(1), {"height": height + 1})
    c_prev = remote(c_ref.at[pl.ds(0, 2)], ch, halo(2), {"tm": tm - 1})
    so_next = remote(so.at[pl.ds(frames - 2, 2)], soh, halo(3), {"tm": tm + 1})
    fg_up = remote(fg.at[:, 0], fgh.at[1], halo(4), {"height": height - 1})
    fg_down = remote(fg.at[:, rows - 1], fgh.at[0], halo(5), {"height": height + 1})

    pl.when(has_prev)(c_prev.start)
    pl.when(has_up)(x_up.start)
    pl.when(has_down)(x_down.start)

    def taps(buf, part, value, count, flip):
        value = value.reshape(-1, chan)
        before, after = shifted(value, cols)
        if flip:
            before, after = after, before
        for j, v in enumerate((before, value, after)):
            v = v.astype(BF16).reshape(frames, count, cols, chan)
            buf[:, part : part + count, :, j * chan : (j + 1) * chan] = v

    def activation(v):
        v = v.astype(F32)
        return (v * sigmoid(v)).astype(BF16).astype(F32)

    taps(s_buf, 1, activation(x_ref[...]), rows, False)

    @pl.when(has_up)
    def _():
        x_down.wait_recv()

    @pl.when(jnp.logical_not(has_up))
    def _():
        xh[0] = jnp.zeros((frames, cols, chan), BF16)

    @pl.when(has_down)
    def _():
        x_up.wait_recv()

    @pl.when(jnp.logical_not(has_down))
    def _():
        xh[1] = jnp.zeros((frames, cols, chan), BF16)

    taps(s_buf, 0, activation(xh[0]), 1, False)
    taps(s_buf, rows + 1, activation(xh[1]), 1, False)

    def s_rows(i):
        return s_buf[:, i : i + rows].reshape(cells, 3 * chan)

    out = dot_nn(s_rows(0), ws_ref[0])
    out += dot_nn(s_rows(1), ws_ref[1])
    out += dot_nn(s_rows(2), ws_ref[2])
    so[...] = out.astype(BF16).reshape(frames, rows, cols, chan)
    pl.when(has_next)(so_next.start)

    @pl.when(has_next)
    def _():
        c_prev.wait_recv()

    @pl.when(jnp.logical_not(has_next))
    def _():
        ch[...] = jnp.zeros(ch.shape, BF16)

    def later(offset):
        if offset == 0:
            return c_ref[...].reshape(cells, chan)
        parts = [c_ref[offset:], ch[:offset]]
        return jnp.concatenate(parts, axis=0).reshape(cells, chan)

    fg_sum = dot_nt(later(0), wt_ref[2])
    fg_sum += dot_nt(later(1), wt_ref[1])
    fg_sum += dot_nt(later(2), wt_ref[0])
    fg[...] = fg_sum.astype(BF16).reshape(frames, rows, cols, chan)

    @pl.when(tm == 0)
    def _():
        c0 = c_ref[0].reshape(-1, chan)
        c1 = c_ref[1].reshape(-1, chan)
        fold = dot_nt(c0, wt_ref[0]) + dot_nt(c0, wt_ref[1]) + dot_nt(c1, wt_ref[0])
        fg[0] = (fg_sum[: rows * cols] + fold).astype(BF16).reshape(rows, cols, chan)

    pl.when(has_up)(fg_up.start)
    pl.when(has_down)(fg_down.start)

    def tap_term(tap):
        if tap < 9:
            i, j = tap // 3, tap % 3
            left = s_buf[:, i : i + rows, :, j * chan : (j + 1) * chan].reshape(cells, chan)
            return dot_tn(left, fg[...].reshape(cells, chan))
        return dot_tn(so[...].reshape(cells, chan), later(2 - (tap - 9)))

    def sum_copy(g, step):
        axis, distance, _ = group_plans[g][step]
        at, size = spots[step]
        place = (g, pl.ds(at, size))
        sems = (sum_send.at[g, step], sum_recv.at[g, step])
        return remote(sb.at[place], rb.at[place], sems, {axis: split_bit(axis, distance)[1]})

    steps = len(group_plans[0])
    halvings = sum(halves for _, _, halves in group_plans[0])
    firsts = [[] for _ in range(GROUPS)]

    def piece(start, size):
        return pl.ds(pl.multiple_of(start, size), size)

    def begin(g):
        bit, _ = split_bit(*group_plans[g][0][:2])
        at, size = spots[0]
        sb[g, at : at + size] = acc[g, piece((1 - bit) * size, size)].astype(BF16)
        sum_copy(g, 0).start()
        firsts[g].append(bit * size)

    def advance(g, step):
        sum_copy(g, step).wait_recv()
        at, size = spots[step]
        halved = group_plans[g][step][2]
        first = firsts[g][-1]
        last = step == steps - 1
        if not last and group_plans[g][step + 1][2]:
            bit, _ = split_bit(*group_plans[g][step + 1][:2])
            next_at, half = spots[step + 1]
            away, kept = (1 - bit) * half, bit * half
            total = acc[g, piece(first + away, half)] + rb[g, piece(at + away, half)].astype(F32)
            sb[g, next_at : next_at + half] = total.astype(BF16)
            sum_copy(g, step + 1).start()
            acc[g, piece(first + kept, half)] += rb[g, piece(at + kept, half)].astype(F32)
            firsts[g].append(first + kept)
            return
        mine = acc[g, piece(first, size)] if halved else sb[g, at : at + size].astype(F32)
        total = (mine + rb[g, at : at + size].astype(F32)).astype(BF16)
        if last:
            full[g, piece(first, size)] = total
            spread(g, halvings - 1).start()
        else:
            next_at, _ = spots[step + 1]
            sb[g, next_at : next_at + size] = total
            sum_copy(g, step + 1).start()

    def spread(g, level):
        axis, distance, _ = group_plans[g][level]
        size = spots[level][1]
        place = full.at[g, piece(firsts[g][level], size)]
        sems = (sum_send.at[g, steps + level], sum_recv.at[g, steps + level])
        return remote(place, place, sems, {axis: split_bit(axis, distance)[1]})

    for g in range(GROUPS):
        for t in range(4):
            acc[g, t * chan : (t + 1) * chan] = tap_term(4 * g + t) * scale
        if g == GROUPS - 1:

            @pl.when(tm == 0)
            def _():
                so0 = so[0].reshape(-1, chan)
                c0 = c_ref[0].reshape(-1, chan)
                c1 = c_ref[1].reshape(-1, chan)
                once = dot_tn(so0, c0) * scale
                acc[g, chan : 2 * chan] += once + dot_tn(so0, c1) * scale
                acc[g, 2 * chan : 3 * chan] += once

        begin(g)

    def make_decoded():
        @pl.when(has_prev)
        def _():
            so_next.wait_recv()

        @pl.when(jnp.logical_not(has_prev))
        def _():
            soh[0] = so[0]
            soh[1] = so[0]

        def earlier(back):
            if back == 0:
                return so[...].reshape(cells, chan)
            parts = [soh[2 - back :], so[: frames - back]]
            return jnp.concatenate(parts, axis=0).reshape(cells, chan)

        total = dot_nn(earlier(0), wt_ref[2])
        total += dot_nn(earlier(1), wt_ref[1])
        total += dot_nn(earlier(2), wt_ref[0])
        total += x_ref[...].astype(F32).reshape(cells, chan)
        dec_ref[...] = total.astype(BF16).reshape(frames, rows, cols, chan)

    def make_grad_taps():
        taps(t_buf, 1, fg[...].astype(F32), rows, True)

        @pl.when(has_up)
        def _():
            fg_down.wait_recv()

        @pl.when(jnp.logical_not(has_up))
        def _():
            fgh[0] = jnp.zeros((frames, cols, chan), BF16)

        @pl.when(has_down)
        def _():
            fg_up.wait_recv()

        @pl.when(jnp.logical_not(has_down))
        def _():
            fgh[1] = jnp.zeros((frames, cols, chan), BF16)

        taps(t_buf, 0, fgh[0].astype(F32), 1, True)
        taps(t_buf, rows + 1, fgh[1].astype(F32), 1, True)

    def make_input_grad():
        total = None
        for i in range(3):
            for j in range(3):
                left = t_buf[:, 2 - i : 2 - i + rows, :, j * chan : (j + 1) * chan]
                term = dot_nt(
                    left.reshape(cells, chan), ws_ref[i, j * chan : (j + 1) * chan]
                )
                total = term if total is None else total + term
        x = x_ref[...].astype(F32).reshape(cells, chan)
        s = sigmoid(x)
        grad = c_ref[...].astype(F32).reshape(cells, chan) + s * (1.0 + x * (1.0 - s)) * total
        ig_ref[...] = grad.astype(BF16).reshape(frames, rows, cols, chan)

    work = [None, make_decoded, make_grad_taps, None]
    for step in range(steps):
        for g in range(GROUPS):
            advance(g, step)
        if step < len(work) and work[step] is not None:
            work[step]()
        if step == steps - 2:
            make_input_grad()
    for level in reversed(range(halvings)):
        for g in range(GROUPS):
            spread(g, level).wait_recv()
            if level > 0:
                spread(g, level - 1).start()

    flat = full[...].reshape(12 * chan, chan)
    sg_ref[...] = flat[: 9 * chan]
    tg_ref[...] = flat[9 * chan :]

    pl.when(has_prev)(c_prev.wait_send)
    pl.when(has_next)(so_next.wait_send)
    for up, down in ((x_up, x_down), (fg_up, fg_down)):
        pl.when(has_up)(up.wait_send)
        pl.when(has_down)(down.wait_send)
    for g in range(GROUPS):
        for step in range(steps):
            sum_copy(g, step).wait_send()
        for level in range(halvings):
            spread(g, level).wait_send()


def local(sizes, frames_in, cotangent, w_spatial, w_temporal):
    x, c = frames_in[0], cotangent[0]
    frames, rows, cols, chan = x.shape
    cell_count = frames * rows * cols * sizes["tm"] * sizes["height"] * sizes["dp"]
    plan = plans(sizes)[0]
    group_rows = 12 * chan // GROUPS
    _, buffer_rows = sums_layout(plan, group_rows)
    exchanges = len(plan) + sum(halves for _, _, halves in plan)
    block = jax.ShapeDtypeStruct(x.shape, BF16)
    vmem = pl.BlockSpec(memory_space=pltpu.VMEM)
    decoded, input_grad, spatial, temporal = pl.pallas_call(
        functools.partial(kernel, sizes, 1.0 / math.sqrt(cell_count)),
        out_shape=(
            block,
            block,
            jax.ShapeDtypeStruct((9 * chan, chan), BF16),
            jax.ShapeDtypeStruct((3 * chan, chan), BF16),
        ),
        in_specs=[vmem] * 4,
        out_specs=(vmem,) * 4,
        scratch_shapes=[
            pltpu.VMEM((2, frames, cols, chan), BF16),
            pltpu.VMEM((2, rows, cols, chan), BF16),
            pltpu.VMEM((2, rows, cols, chan), BF16),
            pltpu.VMEM((2, frames, cols, chan), BF16),
            pltpu.VMEM(x.shape, BF16),
            pltpu.VMEM(x.shape, BF16),
            pltpu.VMEM((frames, rows + 2, cols, 3 * chan), BF16),
            pltpu.VMEM((frames, rows + 2, cols, 3 * chan), BF16),
            pltpu.VMEM((GROUPS, group_rows, chan), F32),
            pltpu.VMEM((GROUPS, buffer_rows, chan), BF16),
            pltpu.VMEM((GROUPS, buffer_rows, chan), BF16),
            pltpu.VMEM((GROUPS, group_rows, chan), BF16),
            pltpu.SemaphoreType.DMA((6,)),
            pltpu.SemaphoreType.DMA((6,)),
            pltpu.SemaphoreType.DMA((GROUPS, exchanges)),
            pltpu.SemaphoreType.DMA((GROUPS, exchanges)),
        ],
        compiler_params=pltpu.CompilerParams(
            collective_id=0, has_side_effects=True, vmem_limit_bytes=48 * 1024 * 1024
        ),
    )(x, c, w_spatial.reshape(3, 3 * chan, chan), w_temporal)
    return (
        decoded[None],
        input_grad[None],
        spatial.reshape(3, 3, chan, chan),
        temporal.reshape(3, chan, chan),
    )


def solution(mesh):
    sizes = dict(mesh.shape)
    spec = P("dp", "tm", "height", None, None)
    return jax.shard_map(
        functools.partial(local, sizes),
        mesh=mesh,
        in_specs=(spec, spec, P(), P()),
        out_specs=(spec, spec, P(), P()),
        check_vma=False,
    )
```

time: 143 us -> 54.7 us (0.38)
  blocking collectives: 82.3 us -> 0 us
  Pallas kernels: 0 us -> 46.3 us
  local copies, waits for them, and re-layouts: 25.6 us -> 7.5 us
  starting transfers between devices: 13.5 us -> 0 us
  waiting for transfers between devices: 9.45 us -> 0 us
  matrix products: 6.2 us -> 0 us
  other arithmetic: 3.42 us -> 0 us
    psum x1 -> x0, blocking collectives: 82.3 us -> none  [local(): summed = lax.psum(weight_terms, ('tm', 'height', 'dp')).astype(jnp.bfloat16)]
    pallas_call x0 -> x1, Pallas kernels: none -> 46.3 us  [local(): pl.pallas_call(functools.partial(kernel, sizes, 1.0 / math.sqrt(cell_coun...]
    ppermute x6 -> x0, starting transfers between devices: 13.5 us -> none  [the longest x2 5.65 us: extended(): before = lax.ppermute(last, axis, up)]
    ppermute x6 -> x0, waiting for transfers between devices: 9.45 us -> none  [the longest x2 7.49 us: extended(): after = lax.ppermute(initial, axis, down)]
    unnamed x58 -> x12, local copies, waits for them, and re-layouts: 16.9 us -> 7.5 us
    slice x11 -> x0, local copies, waits for them, and re-layouts: 7.76 us -> none  [the longest x1 2.48 us: local(): spatial_grad = summed[:9 * channels].reshape(3, 3, channels, channels)]
    dot_general x6 -> x0, matrix products: 6.2 us -> none  [the longest x2 2.22 us: flat_dot(): jnp.dot(left_side.reshape(-1, left_side.shape[-1]), right_side, preferred...]
  transfers between devices with their start and end apart: 6 -> 0, of which waited for: 5 -> 0; matrix products, arithmetic and copies ran while one was open for 12% -> 0% of each run, Pallas kernels for 0% -> 0%
where the time goes in v1:
time: 54.7 us; the launch traced here: 54.5 us
  Pallas kernels  46.3 us (85%)
  local copies, waits for them, and re-layouts  7.5 us (14%)
  between operations  0.65 us (1%)
    pallas_call x1, Pallas kernels, local(): pl.pallas_call(functools.partial(kernel, sizes, 1.0 / math.sqrt(cell_coun...  46.3 us
    unnamed x12, local copies, waits for them, and re-layouts  7.5 us

profile of v1, /device:TPU:1, one launch (start us, length us, event | category | flops | bytes accessed | tf_op | source)
XLA Modules:
  0.0 54.5 jit_solution(1724042489898012974)
XLA Ops:
  0.6 0.0 copy-start
  0.6 1.3 %copy-done = bf16[3,3,256,256]{3,2,1,0:T(8,128)(2,1)S(1)} copy-done((bf16[3,3,256,256]{3,2,1,0:T(8,128)(2,1)S(1)}, bf16[3,3,256,256]{3,2,1,0:T(8,128)(2,1)}, u32[]{:S(2)}) %copy-start) | copy-done | bytes 1179672
  1.9 0.0 copy-start.1
  1.9 1.0 %copy-done.1 = bf16[1,4,4,48,256]{4,3,2,1,0:T(8,128)(2,1)S(1)} copy-done((bf16[1,4,4,48,256]{4,3,2,1,0:T(8,128)(2,1)S(1)}, bf16[1,4,4,48,256]{4,3,2,1,0:T(8,128)(2,1)}, u32[]{:S(2)}) %copy-start.1) | copy-done | bytes 393240
  2.9 0.0 copy-start.2
  2.9 1.0 %copy-done.2 = bf16[1,4,4,48,256]{4,3,2,1,0:T(8,128)(2,1)S(1)} copy-done((bf16[1,4,4,48,256]{4,3,2,1,0:T(8,128)(2,1)S(1)}, bf16[1,4,4,48,256]{4,3,2,1,0:T(8,128)(2,1)}, u32[]{:S(2)}) %copy-start.2) | copy-done | bytes 393240
  3.9 0.0 copy-start.3
  3.9 1.0 %copy-done.3 = bf16[3,256,256]{2,1,0:T(8,128)(2,1)S(1)} copy-done((bf16[3,256,256]{2,1,0:T(8,128)(2,1)S(1)}, bf16[3,256,256]{2,1,0:T(8,128)(2,1)}, u32[]{:S(2)}) %copy-start.3) | copy-done | bytes 393240
  4.9 46.3 %shard_map.75 = (bf16[4,4,48,256]{3,2,1,0:T(8,128)(2,1)S(1)}, bf16[4,4,48,256]{3,2,1,0:T(8,128)(2,1)S(1)}, bf16[2304,256]{1,0:T(8,128)(2,1)S(1)}, bf16[768,256]{1,0:T(8,128)(2,1)S(1)}) custom-call(bf16[4,4,48,256]{3,2,1,0:T(8,128)(2,1)S(1)} %bitcast.9, bf16[4,4,48,256]{3,2,1,0:T(8,128)(2,1)S(1)} %bitcast.10, bf16[3,768,256]{2,1,0:T(8,128)(2,1)S(1)} %bitcast.7, ...), custom_call_target="tpu_custom_call" | custom-call | tf_op jit(solution)/shard_map/pallas_call | solution.py:372
  51.2 0.7 %copy.12 = bf16[1,4,4,48,256]{4,3,2,1,0:T(8,128)(2,1)} copy(bf16[1,4,4,48,256]{4,3,2,1,0:T(8,128)(2,1)S(1)} %bitcast.13) | data formatting | bytes 786432
  52.0 0.7 %copy.13 = bf16[1,4,4,48,256]{4,3,2,1,0:T(8,128)(2,1)} copy(bf16[1,4,4,48,256]{4,3,2,1,0:T(8,128)(2,1)S(1)} %bitcast.12) | data formatting | bytes 786432
  52.7 1.0 %copy.14 = bf16[3,3,256,256]{3,2,1,0:T(8,128)(2,1)} copy(bf16[3,3,256,256]{3,2,1,0:T(8,128)(2,1)S(1)} %bitcast.8) | data formatting | bytes 2359296
  53.7 0.7 %copy.15 = bf16[3,256,256]{2,1,0:T(8,128)(2,1)} copy(bf16[3,256,256]{2,1,0:T(8,128)(2,1)S(1)} %bitcast.11) | data formatting | bytes 786432
Async XLA Ops:
  0.6 1.3 %copy-start = (bf16[3,3,256,256]{3,2,1,0:T(8,128)(2,1)S(1)}, bf16[3,3,256,256]{3,2,1,0:T(8,128)(2,1)}, u32[]{:S(2)}) copy-start(bf16[3,3,256,256]{3,2,1,0:T(8,128)(2,1)} %param.6) | copy-start | bytes 3538948
  1.9 1.0 %copy-start.1 = (bf16[1,4,4,48,256]{4,3,2,1,0:T(8,128)(2,1)S(1)}, bf16[1,4,4,48,256]{4,3,2,1,0:T(8,128)(2,1)}, u32[]{:S(2)}) copy-start(bf16[1,4,4,48,256]{4,3,2,1,0:T(8,128)(2,1)} %param.4) | copy-start | bytes 1179652
  2.9 1.0 %copy-start.2 = (bf16[1,4,4,48,256]{4,3,2,1,0:T(8,128)(2,1)S(1)}, bf16[1,4,4,48,256]{4,3,2,1,0:T(8,128)(2,1)}, u32[]{:S(2)}) copy-start(bf16[1,4,4,48,256]{4,3,2,1,0:T(8,128)(2,1)} %param.5) | copy-start | bytes 1179652
  3.9 1.0 %copy-start.3 = (bf16[3,256,256]{2,1,0:T(8,128)(2,1)S(1)}, bf16[3,256,256]{2,1,0:T(8,128)(2,1)}, u32[]{:S(2)}) copy-start(bf16[3,256,256]{2,1,0:T(8,128)(2,1)} %wt_ref.1) | copy-start | bytes 1179652

commit v2 on v1

--- a/solution.py
+++ b/solution.py
@@ -10,7 +10,8 @@
 
 F32 = jnp.float32
 BF16 = jnp.bfloat16
-GROUPS = 3
+GROUPS = 6
+VMEM_LIMIT = 60 * 1024 * 1024
 
 
 def split_bit(axis, distance):
@@ -29,7 +30,8 @@
     ]
     result = []
     for g in range(GROUPS):
-        order = [("dp", 1)] + near[g:] + near[:g]
+        turn = g % len(near)
+        order = [("dp", 1)] + near[turn:] + near[:turn]
         result.append([(a, d, True) for a, d in order] + [(a, d, False) for a, d in rest])
     return result
 
@@ -69,21 +71,31 @@
 
 def kernel(
     sizes, scale,
-    x_ref, c_ref, ws_ref, wt_ref,
-    dec_ref, ig_ref, sg_ref, tg_ref,
-    xh, ch, soh, fgh, so, fg, s_buf, t_buf, acc, sb, rb, full,
-    halo_send, halo_recv, sum_send, sum_recv,
+    x_hbm, c_hbm, ws_hbm, wt_hbm,
+    dec_hbm, ig_hbm, sg_hbm, tg_hbm,
+    dec_ref, ig_ref,    x_ref, c_ref, ws_ref, wt_ref, xh, ch, soh, fgh, so, fg, s_buf, t_buf, acc, sb, rb, full,
+    load_sem, store_sem, halo_send, halo_recv, sum_send, sum_recv,
 ):
     frames, rows, cols, chan = x_ref.shape
     cells = frames * rows * cols
     tm, height = lax.axis_index("tm"), lax.axis_index("height")
     n_tm, n_h = sizes["tm"], sizes["height"]
     group_plans = plans(sizes)
-    group_rows = 12 * chan // GROUPS
+    per_group = 12 // GROUPS
+    group_rows = per_group * chan
     spots, _ = sums_layout(group_plans[0], group_rows)
 
     has_prev, has_next = tm > 0, tm < n_tm - 1
     has_up, has_down = height > 0, height < n_h - 1
+
+    loads = [
+        pltpu.make_async_copy(src, dst, load_sem.at[n])
+        for n, (src, dst) in enumerate(
+            ((x_hbm, x_ref), (ws_hbm, ws_ref), (c_hbm, c_ref), (wt_hbm, wt_ref))
+        )
+    ]
+    for load in loads:
+        load.start()
 
     barrier = pltpu.get_barrier_semaphore()
 
@@ -111,9 +123,9 @@
     def halo(at):
         return halo_send.at[at], halo_recv.at[at]
 
-    x_up = remote(x_ref.at[:, 0], xh.at[1], halo(0), {"height": height - 1})
-    x_down = remote(x_ref.at[:, rows - 1], xh.at[0], halo(1), {"height": height + 1})
-    c_prev = remote(c_ref.at[pl.ds(0, 2)], ch, halo(2), {"tm": tm - 1})
+    x_up = remote(x_hbm.at[:, 0], xh.at[1], halo(0), {"height": height - 1})
+    x_down = remote(x_hbm.at[:, rows - 1], xh.at[0], halo(1), {"height": height + 1})
+    c_prev = remote(c_hbm.at[pl.ds(0, 2)], ch, halo(2), {"tm": tm - 1})
     so_next = remote(so.at[pl.ds(frames - 2, 2)], soh, halo(3), {"tm": tm + 1})
     fg_up = remote(fg.at[:, 0], fgh.at[1], halo(4), {"height": height - 1})
     fg_down = remote(fg.at[:, rows - 1], fgh.at[0], halo(5), {"height": height + 1})
@@ -135,7 +147,10 @@
         v = v.astype(F32)
         return (v * sigmoid(v)).astype(BF16).astype(F32)
 
+    loads[0].wait()
     taps(s_buf, 1, activation(x_ref[...]), rows, False)
+    for load in loads[1:]:
+        load.wait()
 
     @pl.when(has_up)
     def _():
@@ -256,20 +271,30 @@
         return remote(place, place, sems, {axis: split_bit(axis, distance)[1]})
 
     for g in range(GROUPS):
-        for t in range(4):
-            acc[g, t * chan : (t + 1) * chan] = tap_term(4 * g + t) * scale
-        if g == GROUPS - 1:
-
-            @pl.when(tm == 0)
-            def _():
-                so0 = so[0].reshape(-1, chan)
-                c0 = c_ref[0].reshape(-1, chan)
-                c1 = c_ref[1].reshape(-1, chan)
-                once = dot_tn(so0, c0) * scale
-                acc[g, chan : 2 * chan] += once + dot_tn(so0, c1) * scale
-                acc[g, 2 * chan : 3 * chan] += once
+        for t in range(per_group):
+            tap = per_group * g + t
+            acc[g, t * chan : (t + 1) * chan] = tap_term(tap) * scale
+            if tap in (9, 10):
+
+                @pl.when(tm == 0)
+                def _():
+                    so0 = so[0].reshape(-1, chan)
+                    extra = dot_tn(so0, c_ref[0].reshape(-1, chan))
+                    if tap == 9:
+                        extra += dot_tn(so0, c_ref[1].reshape(-1, chan))
+                    acc[g, t * chan : (t + 1) * chan] += extra * scale
 
         begin(g)
+
+    store_dec = pltpu.make_async_copy(dec_ref, dec_hbm, store_sem.at[0])
+    store_ig = pltpu.make_async_copy(ig_ref, ig_hbm, store_sem.at[1])
+
+    def store_tap(tap):
+        g, t = tap // per_group, tap % per_group
+        to = sg_hbm.at[tap] if tap < 9 else tg_hbm.at[tap - 9]
+        return pltpu.make_async_copy(
+            full.at[g, t * chan : (t + 1) * chan], to, store_sem.at[2 + tap]
+        )
 
     def make_decoded():
         @pl.when(has_prev)
@@ -292,6 +317,7 @@
         total += dot_nn(earlier(2), wt_ref[0])
         total += x_ref[...].astype(F32).reshape(cells, chan)
         dec_ref[...] = total.astype(BF16).reshape(frames, rows, cols, chan)
+        store_dec.start()
 
     def make_grad_taps():
         taps(t_buf, 1, fg[...].astype(F32), rows, True)
@@ -328,6 +354,7 @@
         s = sigmoid(x)
         grad = c_ref[...].astype(F32).reshape(cells, chan) + s * (1.0 + x * (1.0 - s)) * total
         ig_ref[...] = grad.astype(BF16).reshape(frames, rows, cols, chan)
+        store_ig.start()
 
     work = [None, make_decoded, make_grad_taps, None]
     for step in range(steps):
@@ -342,10 +369,9 @@
             spread(g, level).wait_recv()
             if level > 0:
                 spread(g, level - 1).start()
-
-    flat = full[...].reshape(12 * chan, chan)
-    sg_ref[...] = flat[: 9 * chan]
-    tg_ref[...] = flat[9 * chan :]
+            else:
+                for t in range(per_group):
+                    store_tap(per_group * g + t).start()
 
     pl.when(has_prev)(c_prev.wait_send)
     pl.when(has_next)(so_next.wait_send)
@@ -357,6 +383,20 @@
             sum_copy(g, step).wait_send()
         for level in range(halvings):
             spread(g, level).wait_send()
+    store_dec.wait()
+    store_ig.wait()
+    for tap in range(12):
+        store_tap(tap).wait()
+
+
+def write_out(dec_in, ig_in, sg_in, tg_in, dec_out, ig_out, sg_out, tg_out, sem):
+    pairs = [(dec_in, dec_out), (ig_in, ig_out), (tg_in, tg_out)]
+    pairs += [(sg_in.at[3 * i : 3 * i + 3], sg_out.at[3 * i : 3 * i + 3]) for i in range(3)]
+    copies = [pltpu.make_async_copy(a, b, sem.at[n]) for n, (a, b) in enumerate(pairs)]
+    for copy in copies:
+        copy.start()
+    for copy in copies:
+        copy.wait()
 
 
 def local(sizes, frames_in, cotangent, w_spatial, w_temporal):
@@ -368,18 +408,24 @@
     _, buffer_rows = sums_layout(plan, group_rows)
     exchanges = len(plan) + sum(halves for _, _, halves in plan)
     block = jax.ShapeDtypeStruct(x.shape, BF16)
-    vmem = pl.BlockSpec(memory_space=pltpu.VMEM)
-    decoded, input_grad, spatial, temporal = pl.pallas_call(
+    hbm = pl.BlockSpec(memory_space=pltpu.HBM)
+    results = pl.pallas_call(
         functools.partial(kernel, sizes, 1.0 / math.sqrt(cell_count)),
         out_shape=(
             block,
             block,
-            jax.ShapeDtypeStruct((9 * chan, chan), BF16),
-            jax.ShapeDtypeStruct((3 * chan, chan), BF16),
+            jax.ShapeDtypeStruct((9, chan, chan), BF16),
+            jax.ShapeDtypeStruct((3, chan, chan), BF16),
         ),
-        in_specs=[vmem] * 4,
-        out_specs=(vmem,) * 4,
+        in_specs=[hbm] * 4,
+        out_specs=(hbm,) * 4,
         scratch_shapes=[
+            pltpu.VMEM(x.shape, BF16),
+            pltpu.VMEM(x.shape, BF16),
+            pltpu.VMEM(x.shape, BF16),
+            pltpu.VMEM(x.shape, BF16),
+            pltpu.VMEM((3, 3 * chan, chan), BF16),
+            pltpu.VMEM(w_temporal.shape, BF16),
             pltpu.VMEM((2, frames, cols, chan), BF16),
             pltpu.VMEM((2, rows, cols, chan), BF16),
             pltpu.VMEM((2, rows, cols, chan), BF16),
@@ -392,15 +438,25 @@
             pltpu.VMEM((GROUPS, buffer_rows, chan), BF16),
             pltpu.VMEM((GROUPS, buffer_rows, chan), BF16),
             pltpu.VMEM((GROUPS, group_rows, chan), BF16),
+            pltpu.SemaphoreType.DMA((4,)),
+            pltpu.SemaphoreType.DMA((14,)),
             pltpu.SemaphoreType.DMA((6,)),
             pltpu.SemaphoreType.DMA((6,)),
             pltpu.SemaphoreType.DMA((GROUPS, exchanges)),
             pltpu.SemaphoreType.DMA((GROUPS, exchanges)),
         ],
         compiler_params=pltpu.CompilerParams(
-            collective_id=0, has_side_effects=True, vmem_limit_bytes=48 * 1024 * 1024
+            collective_id=0, has_side_effects=True, vmem_limit_bytes=VMEM_LIMIT
         ),
     )(x, c, w_spatial.reshape(3, 3 * chan, chan), w_temporal)
+    decoded, input_grad, spatial, temporal = pl.pallas_call(
+        write_out,
+        out_shape=tuple(jax.ShapeDtypeStruct(r.shape, r.dtype) for r in results),
+        in_specs=[hbm] * 4,
+        out_specs=(hbm,) * 4,
+        scratch_shapes=[pltpu.SemaphoreType.DMA((6,))],
+        compiler_params=pltpu.CompilerParams(vmem_limit_bytes=VMEM_LIMIT),
+    )(*results)
     return (
         decoded[None],
         input_grad[None],

time: 54.7 us -> 119 us (2.18)
  Pallas kernels: 46.3 us -> 118 us
  local copies, waits for them, and re-layouts: 7.5 us -> 0 us
    pallas_call x0 -> x1, Pallas kernels: none -> 72.6 us  [local(): pl.pallas_call(write_out, out_shape=tuple((jax.ShapeDtypeStruct(r.shape,...]
    unnamed x12 -> x0, local copies, waits for them, and re-layouts: 7.5 us -> none
where the time goes in v2:
time: 119 us
  Pallas kernels  118 us (99%)
    pallas_call x1, Pallas kernels, local(): pl.pallas_call(write_out, out_shape=tuple((jax.ShapeDtypeStruct(r.shape,...  72.6 us
    pallas_call x1, Pallas kernels, local(): pl.pallas_call(functools.partial(kernel, sizes, 1.0 / math.sqrt(cell_coun...  45.3 us

profile of v2, /device:TPU:1, one launch (start us, length us, event | category | flops | bytes accessed | tf_op | source)
XLA Modules:
  0.0 118.6 jit_solution(17498900774002698257)
XLA Ops:
  0.6 45.3 %shard_map.75 = (bf16[4,4,48,256]{3,2,1,0:T(8,128)(2,1)}, bf16[4,4,48,256]{3,2,1,0:T(8,128)(2,1)}, bf16[9,256,256]{2,1,0:T(8,128)(2,1)}, bf16[3,256,256]{2,1,0:T(8,128)(2,1)}) custom-call(bf16[4,4,48,256]{3,2,1,0:T(8,128)(2,1)} %bitcast.7, bf16[4,4,48,256]{3,2,1,0:T(8,128)(2,1)} %bitcast.8, bf16[3,768,256]{2,1,0:T(8,128)(2,1)} %bitcast.6, ...), custom_call_target="tpu_custom_call" | custom-call | tf_op jit(solution)/shard_map/pallas_call | solution.py:412
  46.0 72.6 %shard_map.76 = (bf16[4,4,48,256]{3,2,1,0:T(8,128)(2,1)}, bf16[4,4,48,256]{3,2,1,0:T(8,128)(2,1)}, bf16[9,256,256]{2,1,0:T(8,128)(2,1)}, bf16[3,256,256]{2,1,0:T(8,128)(2,1)}) custom-call(bf16[4,4,48,256]{3,2,1,0:T(8,128)(2,1)} %get-tuple-element.12.dec_in, bf16[4,4,48,256]{3,2,1,0:T(8,128)(2,1)} %get-tuple-element.13.ig_in, ...), custom_call_target="tpu_custom_call" | custom-call | tf_op jit(solution)/shard_map/pallas_call | solution.py:452

commit v3 on v2

v3 whole, which is shorter than its diff:
```python
import functools
import math

import jax
import jax.numpy as jnp
from jax import lax
from jax.experimental import pallas as pl
from jax.experimental.pallas import tpu as pltpu
from jax.sharding import PartitionSpec as P

F32 = jnp.float32
BF16 = jnp.bfloat16
GROUPS = 6
VMEM_LIMIT = 60 * 1024 * 1024


def split_bit(axis, distance):
    return lax.rem(lax.div(lax.axis_index(axis), distance), 2)


def across(*flips):
    place = {}
    for axis, distance in flips:
        index = place.get(axis, lax.axis_index(axis))
        place[axis] = index + distance - 2 * distance * split_bit(axis, distance)
    return place


NEAR = (("tm", 1), ("height", 1), ("tm", 2))


def far_bits(sizes):
    return [
        (axis, 1 << b)
        for axis in ("tm", "height")
        for b in range(sizes[axis].bit_length() - 1)
        if (axis, 1 << b) not in NEAR
    ]


def near_order(g):
    turn = g % len(NEAR)
    return NEAR[turn:] + NEAR[:turn]


def sigmoid(v):
    return 1.0 / (1.0 + jnp.exp(-v))


def shifted(v, cols):
    cells, ch = v.shape
    col = lax.broadcasted_iota(jnp.int32, (cells // cols, cols, ch), 1).reshape(cells, ch)
    before = jnp.where(col == 0, 0.0, pltpu.roll(v, 1, 0))
    after = jnp.where(col == cols - 1, 0.0, pltpu.roll(v, cells - 1, 0))
    return before, after


def dot_nn(a, b):
    return jnp.dot(a, b, preferred_element_type=F32)


def dot_nt(a, b):
    return lax.dot_general(a, b, (((1,), (1,)), ((), ())), preferred_element_type=F32)


def dot_tn(a, b):
    return lax.dot_general(a, b, (((0,), (0,)), ((), ())), preferred_element_type=F32)


def kernel(
    sizes, scale,
    x_hbm, c_hbm, ws_hbm, wt_hbm,
    dec_hbm, ig_hbm, sg_hbm, tg_hbm,
    dec_ref, ig_ref,    x_ref, c_ref, ws_ref, wt_ref, xh, ch, soh, fgh, so, fg, s_buf, t_buf, acc, sb, rb, full,
    load_sem, store_sem, halo_send, halo_recv, sum_send, sum_recv,
):
    frames, rows, cols, chan = x_ref.shape
    cells = frames * rows * cols
    tm, height = lax.axis_index("tm"), lax.axis_index("height")
    n_tm, n_h = sizes["tm"], sizes["height"]
    far = far_bits(sizes)
    per_group = 12 // GROUPS
    group_rows = per_group * chan
    half, quarter, own = group_rows // 2, group_rows // 4, group_rows // 16

    has_prev, has_next = tm > 0, tm < n_tm - 1
    has_up, has_down = height > 0, height < n_h - 1

    loads = [
        pltpu.make_async_copy(src, dst, load_sem.at[n])
        for n, (src, dst) in enumerate(
            ((x_hbm, x_ref), (ws_hbm, ws_ref), (c_hbm, c_ref), (wt_hbm, wt_ref))
        )
    ]
    for load in loads:
        load.start()

    barrier = pltpu.get_barrier_semaphore()

    def greet(device):
        pl.semaphore_signal(barrier, inc=1, device_id=device, device_id_type=pl.DeviceIdType.MESH)

    pairs = [(NEAR[0], NEAR[1]), (NEAR[1], NEAR[2]), (NEAR[2], NEAR[0])]
    partners = [(bit,) for bit in ((("dp", 1),) + NEAR + tuple(far))] + pairs
    for flips in partners:
        greet(across(*flips))
    pl.when(has_prev)(lambda: greet({"tm": tm - 1}))
    pl.when(has_next)(lambda: greet({"tm": tm + 1}))
    pl.when(has_up)(lambda: greet({"height": height - 1}))
    pl.when(has_down)(lambda: greet({"height": height + 1}))
    expected = len(partners) + sum(
        jnp.where(has, 1, 0) for has in (has_prev, has_next, has_up, has_down)
    )
    pl.semaphore_wait(barrier, expected)

    def remote(src, dst, sems, device):
        return pltpu.make_async_remote_copy(
            src_ref=src, dst_ref=dst, send_sem=sems[0], recv_sem=sems[1],
            device_id=device, device_id_type=pl.DeviceIdType.MESH,
        )

    def halo(at):
        return halo_send.at[at], halo_recv.at[at]

    x_up = remote(x_hbm.at[:, 0], xh.at[1], halo(0), {"height": height - 1})
    x_down = remote(x_hbm.at[:, rows - 1], xh.at[0], halo(1), {"height": height + 1})
    c_prev = remote(c_hbm.at[pl.ds(0, 2)], ch, halo(2), {"tm": tm - 1})
    so_next = remote(so.at[pl.ds(frames - 2, 2)], soh, halo(3), {"tm": tm + 1})
    fg_up = remote(fg.at[:, 0], fgh.at[1], halo(4), {"height": height - 1})
    fg_down = remote(fg.at[:, rows - 1], fgh.at[0], halo(5), {"height": height + 1})

    pl.when(has_prev)(c_prev.start)
    pl.when(has_up)(x_up.start)
    pl.when(has_down)(x_down.start)

    def taps(buf, part, value, count, flip):
        value = value.reshape(-1, chan)
        before, after = shifted(value, cols)
        if flip:
            before, after = after, before
        for j, v in enumerate((before, value, after)):
            v = v.astype(BF16).reshape(frames, count, cols, chan)
            buf[:, part : part + count, :, j * chan : (j + 1) * chan] = v

    def activation(v):
        v = v.astype(F32)
        return (v * sigmoid(v)).astype(BF16).astype(F32)

    loads[0].wait()
    taps(s_buf, 1, activation(x_ref[...]), rows, False)
    for load in loads[1:]:
        load.wait()

    @pl.when(has_up)
    def _():
        x_down.wait_recv()

    @pl.when(jnp.logical_not(has_up))
    def _():
        xh[0] = jnp.zeros((frames, cols, chan), BF16)

    @pl.when(has_down)
    def _():
        x_up.wait_recv()

    @pl.when(jnp.logical_not(has_down))
    def _():
        xh[1] = jnp.zeros((frames, cols, chan), BF16)

    taps(s_buf, 0, activation(xh[0]), 1, False)
    taps(s_buf, rows + 1, activation(xh[1]), 1, False)

    def s_rows(i):
        return s_buf[:, i : i + rows].reshape(cells, 3 * chan)

    out = dot_nn(s_rows(0), ws_ref[0])
    out += dot_nn(s_rows(1), ws_ref[1])
    out += dot_nn(s_rows(2), ws_ref[2])
    so[...] = out.astype(BF16).reshape(frames, rows, cols, chan)
    pl.when(has_next)(so_next.start)

    def put_term(tap, term):
        g, t = tap // per_group, tap % per_group
        acc[g, t * chan : (t + 1) * chan] = term * scale
        if tap in (9, 10):

            @pl.when(tm == 0)
            def _():
                so0 = so[0].reshape(-1, chan)
                extra = dot_tn(so0, c_ref[0].reshape(-1, chan))
                if tap == 9:
                    extra += dot_tn(so0, c_ref[1].reshape(-1, chan))
                acc[g, t * chan : (t + 1) * chan] += extra * scale

    def temporal_term(tap):
        put_term(tap, dot_tn(so[...].reshape(cells, chan), later(2 - (tap - 9))))

    def spatial_term(tap):
        i, j = tap // 3, tap % 3
        left = s_buf[:, i : i + rows, :, j * chan : (j + 1) * chan].reshape(cells, chan)
        put_term(tap, dot_tn(left, fg[...].reshape(cells, chan)))

    def later(offset):
        if offset == 0:
            return c_ref[...].reshape(cells, chan)
        parts = [c_ref[offset:], ch[:offset]]
        return jnp.concatenate(parts, axis=0).reshape(cells, chan)

    temporal_term(11)

    @pl.when(has_next)
    def _():
        c_prev.wait_recv()

    @pl.when(jnp.logical_not(has_next))
    def _():
        ch[...] = jnp.zeros(ch.shape, BF16)

    def sum_copy(g, at, size, slot, flips):
        place = (g, pl.ds(at, size))
        sems = (sum_send.at[g, slot], sum_recv.at[g, slot])
        return remote(sb.at[place], rb.at[place], sems, across(*flips))

    def piece(start, size):
        return pl.ds(pl.multiple_of(start, size), size)

    def scatter_copies(g, step):
        first, second, third = near_order(g)
        if step == 0:
            return [sum_copy(g, 0, half, 0, [("dp", 1)])]
        if step == 1:
            return [sum_copy(g, half, quarter, 1, [first])]
        at = half + quarter
        if step == 2:
            return [
                sum_copy(g, at + n * own, own, 2 + n, flips)
                for n, flips in enumerate(([second], [third], [second, third]))
            ]
        return [sum_copy(g, at + step * own, own, 2 + step, [far[step - 3]])]

    steps = 3 + len(far)

    def kept(g):
        first, second, third = near_order(g)
        at_dp = split_bit("dp", 1) * half
        at_near = at_dp + split_bit(*first) * quarter
        return at_dp, at_near, at_near + (2 * split_bit(*second) + split_bit(*third)) * own

    def start_all(copies):
        for copy in copies:
            copy.start()

    def begin(g):
        sb[g, :half] = acc[g, piece((1 - split_bit("dp", 1)) * half, half)].astype(BF16)
        start_all(scatter_copies(g, 0))

    def advance(g, step):
        for copy in scatter_copies(g, step):
            copy.wait_recv()
        first, second, third = near_order(g)
        at_dp, at_near, at_own = kept(g)
        if step == 0:
            bit = split_bit(*first)
            away, stay = (1 - bit) * quarter, bit * quarter
            total = acc[g, piece(at_dp + away, quarter)] + rb[g, piece(away, quarter)].astype(F32)
            sb[g, half : half + quarter] = total.astype(BF16)
            start_all(scatter_copies(g, 1))
            acc[g, piece(at_dp + stay, quarter)] += rb[g, piece(stay, quarter)].astype(F32)
        elif step == 1:
            acc[g, piece(at_near, quarter)] += rb[g, half : half + quarter].astype(F32)
            b2, b3 = split_bit(*second), split_bit(*third)
            at = half + quarter
            for n, (p, q) in enumerate(((1 - b2, b3), (b2, 1 - b3), (1 - b2, 1 - b3))):
                away = acc[g, piece(at_near + (2 * p + q) * own, own)]
                sb[g, at + n * own : at + (n + 1) * own] = away.astype(BF16)
            start_all(scatter_copies(g, 2))
        else:
            at = half + quarter
            if step == 2:
                total = acc[g, piece(at_own, own)]
                for n in range(3):
                    total += rb[g, at + n * own : at + (n + 1) * own].astype(F32)
            else:
                here = slice(at + step * own, at + (step + 1) * own)
                total = sb[g, here].astype(F32) + rb[g, here].astype(F32)
            if step < steps - 1:
                sb[g, at + (step + 1) * own : at + (step + 2) * own] = total.astype(BF16)
                start_all(scatter_copies(g, step + 1))
            else:
                full[g, piece(at_own, own)] = total.astype(BF16)
                start_all(gather_copies(g, 0))

    def gather_copies(g, level):
        first, second, third = near_order(g)
        _, at_near, at_own = kept(g)

        def copy(place, slot, flips):
            block = full.at[g, place]
            slot += 2 + steps
            sems = (sum_send.at[g, slot], sum_recv.at[g, slot])
            return remote(block, block, sems, across(*flips))

        if level == 0:
            return [
                copy(piece(at_own, own), n, flips)
                for n, flips in enumerate(([second], [third], [second, third]))
            ]
        if level == 1:
            block = piece(at_near, quarter)
            return [copy(block, 3, [first]), copy(block, 4, [("dp", 1)])]
        other = split_bit("dp", 1) * half + (1 - split_bit(*first)) * quarter
        return [copy(piece(other, quarter), 5, [("dp", 1)])]

    temporal_term(10)
    begin(5)

    fg_sum = dot_nt(later(0), wt_ref[2])
    fg_sum += dot_nt(later(1), wt_ref[1])
    fg_sum += dot_nt(later(2), wt_ref[0])
    fg[...] = fg_sum.astype(BF16).reshape(frames, rows, cols, chan)

    @pl.when(tm == 0)
    def _():
        c0 = c_ref[0].reshape(-1, chan)
        c1 = c_ref[1].reshape(-1, chan)
        fold = dot_nt(c0, wt_ref[0]) + dot_nt(c0, wt_ref[1]) + dot_nt(c1, wt_ref[0])
        fg[0] = (fg_sum[: rows * cols] + fold).astype(BF16).reshape(rows, cols, chan)

    pl.when(has_up)(fg_up.start)
    pl.when(has_down)(fg_down.start)

    temporal_term(9)
    spatial_term(8)
    begin(4)
    for g in range(4):
        spatial_term(2 * g)
        spatial_term(2 * g + 1)
        begin(g)

    store_dec = pltpu.make_async_copy(dec_ref, dec_hbm, store_sem.at[0])
    store_ig = pltpu.make_async_copy(ig_ref, ig_hbm, store_sem.at[1])

    def store_tap(tap):
        g, t = tap // per_group, tap % per_group
        to = sg_hbm.at[tap] if tap < 9 else tg_hbm.at[tap - 9]
        return pltpu.make_async_copy(
            full.at[g, t * chan : (t + 1) * chan], to, store_sem.at[2 + tap]
        )

    def make_decoded(start, count):
        def earlier(back):
            begin_at = start - back
            parts = []
            if begin_at < 0:
                parts.append(soh[2 + begin_at :])
            if begin_at + count > 0:
                parts.append(so[max(begin_at, 0) : begin_at + count])
            value = parts[0] if len(parts) == 1 else jnp.concatenate(parts, axis=0)
            return value.reshape(-1, chan)

        total = dot_nn(earlier(0), wt_ref[2])
        total += dot_nn(earlier(1), wt_ref[1])
        total += dot_nn(earlier(2), wt_ref[0])
        total += x_ref[start : start + count].astype(F32).reshape(-1, chan)
        dec_ref[start : start + count] = total.astype(BF16).reshape(count, rows, cols, chan)

    def decoded_later():
        make_decoded(2, frames - 2)

    def decoded_earlier():
        @pl.when(has_prev)
        def _():
            so_next.wait_recv()

        @pl.when(jnp.logical_not(has_prev))
        def _():
            soh[0] = so[0]
            soh[1] = so[0]

        make_decoded(0, 2)
        store_dec.start()

    def grad_taps_inner():
        taps(t_buf, 1, fg[...].astype(F32), rows, True)

    def grad_taps_outer():
        @pl.when(has_up)
        def _():
            fg_down.wait_recv()

        @pl.when(jnp.logical_not(has_up))
        def _():
            fgh[0] = jnp.zeros((frames, cols, chan), BF16)

        @pl.when(has_down)
        def _():
            fg_up.wait_recv()

        @pl.when(jnp.logical_not(has_down))
        def _():
            fgh[1] = jnp.zeros((frames, cols, chan), BF16)

        taps(t_buf, 0, fgh[0].astype(F32), 1, True)
        taps(t_buf, rows + 1, fgh[1].astype(F32), 1, True)

    def make_input_grad(start, count):
        total = None
        span = slice(start, start + count)
        for i in range(3):
            for j in range(3):
                left = t_buf[span, 2 - i : 2 - i + rows, :, j * chan : (j + 1) * chan]
                term = dot_nt(left.reshape(-1, chan), ws_ref[i, j * chan : (j + 1) * chan])
                total = term if total is None else total + term
        x = x_ref[span].astype(F32).reshape(-1, chan)
        s = sigmoid(x)
        grad = c_ref[span].astype(F32).reshape(-1, chan) + s * (1.0 + x * (1.0 - s)) * total
        ig_ref[span] = grad.astype(BF16).reshape(count, rows, cols, chan)

    def input_grad_first():
        make_input_grad(0, frames // 2)

    def input_grad_second():
        make_input_grad(frames // 2, frames - frames // 2)
        store_ig.start()

    units = [
        decoded_later, grad_taps_inner, decoded_earlier, grad_taps_outer,
        input_grad_first, input_grad_second,
    ]
    order = (5, 4, 0, 1, 2, 3)
    for step in range(steps):
        for n, g in enumerate(order):
            advance(g, step)
            if n in (2, 5) and units:
                units.pop(0)()
    for level in range(3):
        for g in order:
            copies = gather_copies(g, level)
            if level < 2:
                for copy in copies if level == 0 else copies[:1]:
                    copy.wait_recv()
                start_all(gather_copies(g, level + 1))
                continue
            gather_copies(g, 1)[1].wait_recv()
            copies[0].wait_recv()
            for t in range(per_group):
                store_tap(per_group * g + t).start()

    pl.when(has_prev)(c_prev.wait_send)
    pl.when(has_next)(so_next.wait_send)
    for up, down in ((x_up, x_down), (fg_up, fg_down)):
        pl.when(has_up)(up.wait_send)
        pl.when(has_down)(down.wait_send)
    for g in range(GROUPS):
        for step in range(steps):
            for copy in scatter_copies(g, step):
                copy.wait_send()
        for level in range(3):
            for copy in gather_copies(g, level):
                copy.wait_send()
    store_dec.wait()
    store_ig.wait()
    for tap in range(12):
        store_tap(tap).wait()


def write_out(*refs):
    ins, outs, held, sem = refs[:4], refs[4:8], refs[8:12], refs[12]
    parts = [(n, pl.ds(i, 3)) for n in (2, 3) for i in range(0, ins[n].shape[0], 3)]
    parts += [(n, pl.ds(0, ins[n].shape[0])) for n in (0, 1)]

    def copies(source, target, row):
        return [
            pltpu.make_async_copy(source[n].at[at], target[n].at[at], sem.at[row, k])
            for k, (n, at) in enumerate(parts)
        ]

    loads, stores = copies(ins, held, 0), copies(held, outs, 1)
    for load in loads:
        load.start()
    for load, store in zip(loads, stores):
        load.wait()
        store.start()
    for store in stores:
        store.wait()


def local(sizes, frames_in, cotangent, w_spatial, w_temporal):
    x, c = frames_in[0], cotangent[0]
    frames, rows, cols, chan = x.shape
    cell_count = frames * rows * cols * sizes["tm"] * sizes["height"] * sizes["dp"]
    group_rows = 12 * chan // GROUPS
    far = len(far_bits(sizes))
    buffer_rows = group_rows * 3 // 4 + (3 + far) * (group_rows // 16)
    exchanges = 5 + far + 6
    block = jax.ShapeDtypeStruct(x.shape, BF16)
    hbm = pl.BlockSpec(memory_space=pltpu.HBM)
    results = pl.pallas_call(
        functools.partial(kernel, sizes, 1.0 / math.sqrt(cell_count)),
        out_shape=(
            block,
            block,
            jax.ShapeDtypeStruct((9, chan, chan), BF16),
            jax.ShapeDtypeStruct((3, chan, chan), BF16),
        ),
        in_specs=[hbm] * 4,
        out_specs=(hbm,) * 4,
        scratch_shapes=[
            pltpu.VMEM(x.shape, BF16),
            pltpu.VMEM(x.shape, BF16),
            pltpu.VMEM(x.shape, BF16),
            pltpu.VMEM(x.shape, BF16),
            pltpu.VMEM((3, 3 * chan, chan), BF16),
            pltpu.VMEM(w_temporal.shape, BF16),
            pltpu.VMEM((2, frames, cols, chan), BF16),
            pltpu.VMEM((2, rows, cols, chan), BF16),
            pltpu.VMEM((2, rows, cols, chan), BF16),
            pltpu.VMEM((2, frames, cols, chan), BF16),
            pltpu.VMEM(x.shape, BF16),
            pltpu.VMEM(x.shape, BF16),
            pltpu.VMEM((frames, rows + 2, cols, 3 * chan), BF16),
            pltpu.VMEM((frames, rows + 2, cols, 3 * chan), BF16),
            pltpu.VMEM((GROUPS, group_rows, chan), F32),
            pltpu.VMEM((GROUPS, buffer_rows, chan), BF16),
            pltpu.VMEM((GROUPS, buffer_rows, chan), BF16),
            pltpu.VMEM((GROUPS, group_rows, chan), BF16),
            pltpu.SemaphoreType.DMA((4,)),
            pltpu.SemaphoreType.DMA((14,)),
            pltpu.SemaphoreType.DMA((6,)),
            pltpu.SemaphoreType.DMA((6,)),
            pltpu.SemaphoreType.DMA((GROUPS, exchanges)),
            pltpu.SemaphoreType.DMA((GROUPS, exchanges)),
        ],
        compiler_params=pltpu.CompilerParams(
            collective_id=0, has_side_effects=True, vmem_limit_bytes=VMEM_LIMIT
        ),
    )(x, c, w_spatial.reshape(3, 3 * chan, chan), w_temporal)
    decoded, input_grad, spatial, temporal = pl.pallas_call(
        write_out,
        out_shape=tuple(jax.ShapeDtypeStruct(r.shape, r.dtype) for r in results),
        in_specs=[hbm] * 4,
        out_specs=(hbm,) * 4,
        scratch_shapes=[pltpu.VMEM(r.shape, r.dtype) for r in results]
        + [pltpu.SemaphoreType.DMA((2, 6))],
        compiler_params=pltpu.CompilerParams(vmem_limit_bytes=VMEM_LIMIT),
    )(*results)
    return (
        decoded[None],
        input_grad[None],
        spatial.reshape(3, 3, chan, chan),
        temporal.reshape(3, chan, chan),
    )


def solution(mesh):
    sizes = dict(mesh.shape)
    spec = P("dp", "tm", "height", None, None)
    return jax.shard_map(
        functools.partial(local, sizes),
        mesh=mesh,
        in_specs=(spec, spec, P(), P()),
        out_specs=(spec, spec, P(), P()),
        check_vma=False,
    )
```

time: 119 us -> 44.9 us (0.38)
  Pallas kernels: 118 us -> 44.1 us
    pallas_call x1, Pallas kernels: 72.6 us -> 2.49 us  [local(): pl.pallas_call(write_out, out_shape=tuple((jax.ShapeDtypeStruct(r.shape,...]
    pallas_call x1, Pallas kernels: 45.3 us -> 41.7 us  [local(): pl.pallas_call(functools.partial(kernel, sizes, 1.0 / math.sqrt(cell_coun...]
where the time goes in v3:
time: 44.9 us; the launch traced here: 44.8 us
  Pallas kernels  44.1 us (98%)
  between operations  0.64 us (1%)
    pallas_call x1, Pallas kernels, local(): pl.pallas_call(functools.partial(kernel, sizes, 1.0 / math.sqrt(cell_coun...  41.7 us
    pallas_call x1, Pallas kernels, local(): pl.pallas_call(write_out, out_shape=tuple((jax.ShapeDtypeStruct(r.shape,...  2.49 us

profile of v3, /device:TPU:1, one launch (start us, length us, event | category | flops | bytes accessed | tf_op | source)
XLA Modules:
  0.0 44.8 jit_solution(18122340087856459529)
XLA Ops:
  0.6 41.7 %shard_map.75 = (bf16[4,4,48,256]{3,2,1,0:T(8,128)(2,1)}, bf16[4,4,48,256]{3,2,1,0:T(8,128)(2,1)}, bf16[9,256,256]{2,1,0:T(8,128)(2,1)}, bf16[3,256,256]{2,1,0:T(8,128)(2,1)}) custom-call(bf16[4,4,48,256]{3,2,1,0:T(8,128)(2,1)} %bitcast.7, bf16[4,4,48,256]{3,2,1,0:T(8,128)(2,1)} %bitcast.8, bf16[3,768,256]{2,1,0:T(8,128)(2,1)} %bitcast.6, ...), custom_call_target="tpu_custom_call" | custom-call | tf_op jit(solution)/shard_map/pallas_call | solution.py:498
  42.3 2.5 %shard_map.76 = (bf16[4,4,48,256]{3,2,1,0:T(8,128)(2,1)}, bf16[4,4,48,256]{3,2,1,0:T(8,128)(2,1)}, bf16[9,256,256]{2,1,0:T(8,128)(2,1)}, bf16[3,256,256]{2,1,0:T(8,128)(2,1)}) custom-call(bf16[4,4,48,256]{3,2,1,0:T(8,128)(2,1)} %get-tuple-element.12.refs_0_, bf16[4,4,48,256]{3,2,1,0:T(8,128)(2,1)} %get-tuple-element.13.refs_1_, ...), custom_call_target="tpu_custom_call" | custom-call | tf_op jit(solution)/shard_map/pallas_call | solution.py:538

commit v4 on v3

--- a/solution.py
+++ b/solution.py
@@ -71,7 +71,7 @@
     sizes, scale,
     x_hbm, c_hbm, ws_hbm, wt_hbm,
     dec_hbm, ig_hbm, sg_hbm, tg_hbm,
-    dec_ref, ig_ref,    x_ref, c_ref, ws_ref, wt_ref, xh, ch, soh, fgh, so, fg, s_buf, t_buf, acc, sb, rb, full,
+    dec_ref, ig_ref,    x_ref, c_ref, ws_ref, wt_ref, xh, fgh, so, fg, s_buf, t_buf, acc, sb, rb, full,
     load_sem, store_sem, halo_send, halo_recv, sum_send, sum_recv,
 ):
     frames, rows, cols, chan = x_ref.shape
@@ -89,7 +89,7 @@
     loads = [
         pltpu.make_async_copy(src, dst, load_sem.at[n])
         for n, (src, dst) in enumerate(
-            ((x_hbm, x_ref), (ws_hbm, ws_ref), (c_hbm, c_ref), (wt_hbm, wt_ref))
+            ((x_hbm, x_ref), (ws_hbm, ws_ref), (c_hbm, c_ref.at[pl.ds(0, frames)]), (wt_hbm, wt_ref))
         )
     ]
     for load in loads:
@@ -124,8 +124,8 @@
 
     x_up = remote(x_hbm.at[:, 0], xh.at[1], halo(0), {"height": height - 1})
     x_down = remote(x_hbm.at[:, rows - 1], xh.at[0], halo(1), {"height": height + 1})
-    c_prev = remote(c_hbm.at[pl.ds(0, 2)], ch, halo(2), {"tm": tm - 1})
-    so_next = remote(so.at[pl.ds(frames - 2, 2)], soh, halo(3), {"tm": tm + 1})
+    c_prev = remote(c_hbm.at[pl.ds(0, 2)], c_ref.at[pl.ds(frames, 2)], halo(2), {"tm": tm - 1})
+    so_next = remote(so.at[pl.ds(frames, 2)], so.at[pl.ds(0, 2)], halo(3), {"tm": tm + 1})
     fg_up = remote(fg.at[:, 0], fgh.at[1], halo(4), {"height": height - 1})
     fg_down = remote(fg.at[:, rows - 1], fgh.at[0], halo(5), {"height": height + 1})
 
@@ -133,21 +133,24 @@
     pl.when(has_up)(x_up.start)
     pl.when(has_down)(x_down.start)
 
-    def taps(buf, part, value, count, flip):
+    def taps(buf, f, part, value, count, flip):
         value = value.reshape(-1, chan)
         before, after = shifted(value, cols)
         if flip:
             before, after = after, before
         for j, v in enumerate((before, value, after)):
-            v = v.astype(BF16).reshape(frames, count, cols, chan)
-            buf[:, part : part + count, :, j * chan : (j + 1) * chan] = v
+            v = v.astype(BF16).reshape(count, cols, chan)
+            buf[f, part : part + count, :, j * chan : (j + 1) * chan] = v
+
+    def each_frame(body, first=0, last=frames):
+        lax.fori_loop(first, last, lambda f, unused: body(f), None)
 
     def activation(v):
         v = v.astype(F32)
         return (v * sigmoid(v)).astype(BF16).astype(F32)
 
     loads[0].wait()
-    taps(s_buf, 1, activation(x_ref[...]), rows, False)
+    each_frame(lambda f: taps(s_buf, f, 1, activation(x_ref[f]), rows, False))
     for load in loads[1:]:
         load.wait()
 
@@ -167,16 +170,17 @@
     def _():
         xh[1] = jnp.zeros((frames, cols, chan), BF16)
 
-    taps(s_buf, 0, activation(xh[0]), 1, False)
-    taps(s_buf, rows + 1, activation(xh[1]), 1, False)
-
-    def s_rows(i):
-        return s_buf[:, i : i + rows].reshape(cells, 3 * chan)
-
-    out = dot_nn(s_rows(0), ws_ref[0])
-    out += dot_nn(s_rows(1), ws_ref[1])
-    out += dot_nn(s_rows(2), ws_ref[2])
-    so[...] = out.astype(BF16).reshape(frames, rows, cols, chan)
+    def spatial_frame(f):
+        taps(s_buf, f, 0, activation(xh[0, f]), 1, False)
+        taps(s_buf, f, rows + 1, activation(xh[1, f]), 1, False)
+        out = None
+        for i in range(3):
+            left = s_buf[f, i : i + rows].reshape(rows * cols, 3 * chan)
+            term = dot_nn(left, ws_ref[i])
+            out = term if out is None else out + term
+        so[f + 2] = out.astype(BF16).reshape(rows, cols, chan)
+
+    each_frame(spatial_frame)
     pl.when(has_next)(so_next.start)
 
     def put_term(tap, term):
@@ -186,14 +190,14 @@
 
             @pl.when(tm == 0)
             def _():
-                so0 = so[0].reshape(-1, chan)
+                so0 = so[2].reshape(-1, chan)
                 extra = dot_tn(so0, c_ref[0].reshape(-1, chan))
                 if tap == 9:
                     extra += dot_tn(so0, c_ref[1].reshape(-1, chan))
                 acc[g, t * chan : (t + 1) * chan] += extra * scale
 
     def temporal_term(tap):
-        put_term(tap, dot_tn(so[...].reshape(cells, chan), later(2 - (tap - 9))))
+        put_term(tap, dot_tn(so[2:].reshape(cells, chan), later(2 - (tap - 9))))
 
     def spatial_term(tap):
         i, j = tap // 3, tap % 3
@@ -201,10 +205,7 @@
         put_term(tap, dot_tn(left, fg[...].reshape(cells, chan)))
 
     def later(offset):
-        if offset == 0:
-            return c_ref[...].reshape(cells, chan)
-        parts = [c_ref[offset:], ch[:offset]]
-        return jnp.concatenate(parts, axis=0).reshape(cells, chan)
+        return c_ref[offset : offset + frames].reshape(cells, chan)
 
     temporal_term(11)
 
@@ -214,7 +215,7 @@
 
     @pl.when(jnp.logical_not(has_next))
     def _():
-        ch[...] = jnp.zeros(ch.shape, BF16)
+        c_ref[frames:] = jnp.zeros((2, rows, cols, chan), BF16)
 
     def sum_copy(g, at, size, slot, flips):
         place = (g, pl.ds(at, size))
@@ -314,17 +315,22 @@
     temporal_term(10)
     begin(5)
 
-    fg_sum = dot_nt(later(0), wt_ref[2])
-    fg_sum += dot_nt(later(1), wt_ref[1])
-    fg_sum += dot_nt(later(2), wt_ref[0])
-    fg[...] = fg_sum.astype(BF16).reshape(frames, rows, cols, chan)
+    def frame_part(f):
+        total = dot_nt(c_ref[f].reshape(-1, chan), wt_ref[2])
+        total += dot_nt(c_ref[f + 1].reshape(-1, chan), wt_ref[1])
+        return total + dot_nt(c_ref[f + 2].reshape(-1, chan), wt_ref[0])
+
+    def put_frame(f, total):
+        fg[f] = total.astype(BF16).reshape(rows, cols, chan)
+
+    each_frame(lambda f: put_frame(f, frame_part(f)))
 
     @pl.when(tm == 0)
     def _():
         c0 = c_ref[0].reshape(-1, chan)
         c1 = c_ref[1].reshape(-1, chan)
         fold = dot_nt(c0, wt_ref[0]) + dot_nt(c0, wt_ref[1]) + dot_nt(c1, wt_ref[0])
-        fg[0] = (fg_sum[: rows * cols] + fold).astype(BF16).reshape(rows, cols, chan)
+        put_frame(0, frame_part(0) + fold)
 
     pl.when(has_up)(fg_up.start)
     pl.when(has_down)(fg_down.start)
@@ -347,25 +353,14 @@
             full.at[g, t * chan : (t + 1) * chan], to, store_sem.at[2 + tap]
         )
 
-    def make_decoded(start, count):
-        def earlier(back):
-            begin_at = start - back
-            parts = []
-            if begin_at < 0:
-                parts.append(soh[2 + begin_at :])
-            if begin_at + count > 0:
-                parts.append(so[max(begin_at, 0) : begin_at + count])
-            value = parts[0] if len(parts) == 1 else jnp.concatenate(parts, axis=0)
-            return value.reshape(-1, chan)
-
-        total = dot_nn(earlier(0), wt_ref[2])
-        total += dot_nn(earlier(1), wt_ref[1])
-        total += dot_nn(earlier(2), wt_ref[0])
-        total += x_ref[start : start + count].astype(F32).reshape(-1, chan)
-        dec_ref[start : start + count] = total.astype(BF16).reshape(count, rows, cols, chan)
+    def make_decoded(f):
+        total = x_ref[f].astype(F32).reshape(-1, chan)
+        for k in range(3):
+            total += dot_nn(so[f + k].reshape(-1, chan), wt_ref[k])
+        dec_ref[f] = total.astype(BF16).reshape(rows, cols, chan)
 
     def decoded_later():
-        make_decoded(2, frames - 2)
+        each_frame(make_decoded, 2, frames)
 
     def decoded_earlier():
         @pl.when(has_prev)
@@ -374,14 +369,14 @@
 
         @pl.when(jnp.logical_not(has_prev))
         def _():
-            soh[0] = so[0]
-            soh[1] = so[0]
-
-        make_decoded(0, 2)
+            so[0] = so[2]
+            so[1] = so[2]
+
+        each_frame(make_decoded, 0, 2)
         store_dec.start()
 
     def grad_taps_inner():
-        taps(t_buf, 1, fg[...].astype(F32), rows, True)
+        each_frame(lambda f: taps(t_buf, f, 1, fg[f].astype(F32), rows, True))
 
     def grad_taps_outer():
         @pl.when(has_up)
@@ -400,27 +395,29 @@
         def _():
             fgh[1] = jnp.zeros((frames, cols, chan), BF16)
 
-        taps(t_buf, 0, fgh[0].astype(F32), 1, True)
-        taps(t_buf, rows + 1, fgh[1].astype(F32), 1, True)
-
-    def make_input_grad(start, count):
+        def outer(f):
+            taps(t_buf, f, 0, fgh[0, f].astype(F32), 1, True)
+            taps(t_buf, f, rows + 1, fgh[1, f].astype(F32), 1, True)
+
+        each_frame(outer)
+
+    def make_input_grad(f):
         total = None
-        span = slice(start, start + count)
         for i in range(3):
             for j in range(3):
-                left = t_buf[span, 2 - i : 2 - i + rows, :, j * chan : (j + 1) * chan]
+                left = t_buf[f, 2 - i : 2 - i + rows, :, j * chan : (j + 1) * chan]
                 term = dot_nt(left.reshape(-1, chan), ws_ref[i, j * chan : (j + 1) * chan])
                 total = term if total is None else total + term
-        x = x_ref[span].astype(F32).reshape(-1, chan)
+        x = x_ref[f].astype(F32).reshape(-1, chan)
         s = sigmoid(x)
-        grad = c_ref[span].astype(F32).reshape(-1, chan) + s * (1.0 + x * (1.0 - s)) * total
-        ig_ref[span] = grad.astype(BF16).reshape(count, rows, cols, chan)
+        grad = c_ref[f].astype(F32).reshape(-1, chan) + s * (1.0 + x * (1.0 - s)) * total
+        ig_ref[f] = grad.astype(BF16).reshape(rows, cols, chan)
 
     def input_grad_first():
-        make_input_grad(0, frames // 2)
+        each_frame(make_input_grad, 0, frames // 2)
 
     def input_grad_second():
-        make_input_grad(frames // 2, frames - frames // 2)
+        each_frame(make_input_grad, frames // 2, frames)
         store_ig.start()
 
     units = [
@@ -493,6 +490,7 @@
     far = len(far_bits(sizes))
     buffer_rows = group_rows * 3 // 4 + (3 + far) * (group_rows // 16)
     exchanges = 5 + far + 6
+    longer = pltpu.VMEM((frames + 2,) + x.shape[1:], BF16)
     block = jax.ShapeDtypeStruct(x.shape, BF16)
     hbm = pl.BlockSpec(memory_space=pltpu.HBM)
     results = pl.pallas_call(
@@ -509,14 +507,12 @@
             pltpu.VMEM(x.shape, BF16),
             pltpu.VMEM(x.shape, BF16),
             pltpu.VMEM(x.shape, BF16),
-            pltpu.VMEM(x.shape, BF16),
+            longer,
             pltpu.VMEM((3, 3 * chan, chan), BF16),
             pltpu.VMEM(w_temporal.shape, BF16),
             pltpu.VMEM((2, frames, cols, chan), BF16),
-            pltpu.VMEM((2, rows, cols, chan), BF16),
-            pltpu.VMEM((2, rows, cols, chan), BF16),
             pltpu.VMEM((2, frames, cols, chan), BF16),
-            pltpu.VMEM(x.shape, BF16),
+            longer,
             pltpu.VMEM(x.shape, BF16),
             pltpu.VMEM((frames, rows + 2, cols, 3 * chan), BF16),
             pltpu.VMEM((frames, rows + 2, cols, 3 * chan), BF16),

time: 44.9 us -> 45.8 us (1.020)
  Pallas kernels: 44.1 us -> 45 us
    pallas_call x1, Pallas kernels: 41.7 us -> 42.6 us  [local(): pl.pallas_call(functools.partial(kernel, sizes, 1.0 / math.sqrt(cell_coun...]
where the time goes in v4:
time: 45.8 us; the launch traced here: 45.7 us
  Pallas kernels  45 us (98%)
  between operations  0.64 us (1%)
    pallas_call x1, Pallas kernels, local(): pl.pallas_call(functools.partial(kernel, sizes, 1.0 / math.sqrt(cell_coun...  42.6 us
    pallas_call x1, Pallas kernels, local(): pl.pallas_call(write_out, out_shape=tuple((jax.ShapeDtypeStruct(r.shape,...  2.49 us

profile of v4, /device:TPU:1, one launch (start us, length us, event | category | flops | bytes accessed | tf_op | source)
XLA Modules:
  0.0 45.7 jit_solution(15265471764343278289)
XLA Ops:
  0.6 42.6 %shard_map.75 = (bf16[4,4,48,256]{3,2,1,0:T(8,128)(2,1)}, bf16[4,4,48,256]{3,2,1,0:T(8,128)(2,1)}, bf16[9,256,256]{2,1,0:T(8,128)(2,1)}, bf16[3,256,256]{2,1,0:T(8,128)(2,1)}) custom-call(bf16[4,4,48,256]{3,2,1,0:T(8,128)(2,1)} %bitcast.7, bf16[4,4,48,256]{3,2,1,0:T(8,128)(2,1)} %bitcast.8, bf16[3,768,256]{2,1,0:T(8,128)(2,1)} %bitcast.6, ...), custom_call_target="tpu_custom_call" | custom-call | tf_op jit(solution)/shard_map/pallas_call | solution.py:496
  43.2 2.5 %shard_map.76 = (bf16[4,4,48,256]{3,2,1,0:T(8,128)(2,1)}, bf16[4,4,48,256]{3,2,1,0:T(8,128)(2,1)}, bf16[9,256,256]{2,1,0:T(8,128)(2,1)}, bf16[3,256,256]{2,1,0:T(8,128)(2,1)}) custom-call(bf16[4,4,48,256]{3,2,1,0:T(8,128)(2,1)} %get-tuple-element.12.refs_0_, bf16[4,4,48,256]{3,2,1,0:T(8,128)(2,1)} %get-tuple-element.13.refs_1_, ...), custom_call_target="tpu_custom_call" | custom-call | tf_op jit(solution)/shard_map/pallas_call | solution.py:534

commit v5 on v3

--- a/solution.py
+++ b/solution.py
@@ -11,6 +11,7 @@
 F32 = jnp.float32
 BF16 = jnp.bfloat16
 GROUPS = 6
+ORDER = (5, 4, 0, 1, 2, 3)
 VMEM_LIMIT = 60 * 1024 * 1024
 
 
@@ -177,7 +178,6 @@
     out += dot_nn(s_rows(1), ws_ref[1])
     out += dot_nn(s_rows(2), ws_ref[2])
     so[...] = out.astype(BF16).reshape(frames, rows, cols, chan)
-    pl.when(has_next)(so_next.start)
 
     def put_term(tap, term):
         g, t = tap // per_group, tap % per_group
@@ -215,6 +215,8 @@
     @pl.when(jnp.logical_not(has_next))
     def _():
         ch[...] = jnp.zeros(ch.shape, BF16)
+
+    pl.when(has_next)(so_next.start)
 
     def sum_copy(g, at, size, slot, flips):
         place = (g, pl.ds(at, size))
@@ -312,7 +314,7 @@
         return [copy(piece(other, quarter), 5, [("dp", 1)])]
 
     temporal_term(10)
-    begin(5)
+    begin(ORDER[0])
 
     fg_sum = dot_nt(later(0), wt_ref[2])
     fg_sum += dot_nt(later(1), wt_ref[1])
@@ -328,14 +330,6 @@
 
     pl.when(has_up)(fg_up.start)
     pl.when(has_down)(fg_down.start)
-
-    temporal_term(9)
-    spatial_term(8)
-    begin(4)
-    for g in range(4):
-        spatial_term(2 * g)
-        spatial_term(2 * g + 1)
-        begin(g)
 
     store_dec = pltpu.make_async_copy(dec_ref, dec_hbm, store_sem.at[0])
     store_ig = pltpu.make_async_copy(ig_ref, ig_hbm, store_sem.at[1])
@@ -416,35 +410,39 @@
         grad = c_ref[span].astype(F32).reshape(-1, chan) + s * (1.0 + x * (1.0 - s)) * total
         ig_ref[span] = grad.astype(BF16).reshape(count, rows, cols, chan)
 
-    def input_grad_first():
-        make_input_grad(0, frames // 2)
-
-    def input_grad_second():
-        make_input_grad(frames // 2, frames - frames // 2)
-        store_ig.start()
-
-    units = [
-        decoded_later, grad_taps_inner, decoded_earlier, grad_taps_outer,
-        input_grad_first, input_grad_second,
-    ]
-    order = (5, 4, 0, 1, 2, 3)
-    for step in range(steps):
-        for n, g in enumerate(order):
-            advance(g, step)
-            if n in (2, 5) and units:
-                units.pop(0)()
-    for level in range(3):
-        for g in order:
-            copies = gather_copies(g, level)
-            if level < 2:
-                for copy in copies if level == 0 else copies[:1]:
-                    copy.wait_recv()
-                start_all(gather_copies(g, level + 1))
-                continue
-            gather_copies(g, 1)[1].wait_recv()
-            copies[0].wait_recv()
-            for t in range(per_group):
-                store_tap(per_group * g + t).start()
+    def gather(g, level):
+        copies = gather_copies(g, level)
+        if level < 2:
+            for copy in copies if level == 0 else copies[:1]:
+                copy.wait_recv()
+            start_all(gather_copies(g, level + 1))
+            return
+        gather_copies(g, 1)[1].wait_recv()
+        copies[0].wait_recv()
+        for t in range(per_group):
+            store_tap(per_group * g + t).start()
+
+    def terms(g):
+        for tap in range(per_group * g, per_group * g + per_group):
+            temporal_term(tap) if tap >= 9 else spatial_term(tap)
+        begin(g)
+
+    events = []
+    for n, g in enumerate(ORDER):
+        if n > 0:
+            events.append((n, functools.partial(terms, g)))
+        for step in range(steps):
+            after = (2, 5, 8)[step] if step < 3 else 8 + 4 * (step - 2)
+            events.append((n + after + 0.1, functools.partial(advance, g, step)))
+        for level in range(3):
+            after = 8 + 4 * (steps - 3) + 3 * (level + 1)
+            events.append((n + after + 0.2, functools.partial(gather, g, level)))
+    units = [decoded_later, grad_taps_inner, decoded_earlier, grad_taps_outer]
+    units += [functools.partial(make_input_grad, f, 1) for f in range(frames)] + [store_ig.start]
+    for n, unit in enumerate(units):
+        events.append((GROUPS + 0.5 + n, unit))
+    for _, event in sorted(events, key=lambda e: e[0]):
+        event()
 
     pl.when(has_prev)(c_prev.wait_send)
     pl.when(has_next)(so_next.wait_send)

time: 44.9 us -> 44.1 us (0.982)
  Pallas kernels: 44.1 us -> 43.3 us
    pallas_call x1, Pallas kernels: 41.7 us -> 40.8 us  [local(): pl.pallas_call(functools.partial(kernel, sizes, 1.0 / math.sqrt(cell_coun...]
where the time goes in v5:
time: 44.1 us; the launch traced here: 43.9 us
  Pallas kernels  43.3 us (98%)
  between operations  0.64 us (1%)
    pallas_call x1, Pallas kernels, local(): pl.pallas_call(functools.partial(kernel, sizes, 1.0 / math.sqrt(cell_coun...  40.8 us
    pallas_call x1, Pallas kernels, local(): pl.pallas_call(write_out, out_shape=tuple((jax.ShapeDtypeStruct(r.shape,...  2.49 us

profile of v5, /device:TPU:1, one launch (start us, length us, event | category | flops | bytes accessed | tf_op | source)
XLA Modules:
  0.0 43.9 jit_solution(10497641509994595151)
XLA Ops:
  0.6 40.8 %shard_map.75 = (bf16[4,4,48,256]{3,2,1,0:T(8,128)(2,1)}, bf16[4,4,48,256]{3,2,1,0:T(8,128)(2,1)}, bf16[9,256,256]{2,1,0:T(8,128)(2,1)}, bf16[3,256,256]{2,1,0:T(8,128)(2,1)}) custom-call(bf16[4,4,48,256]{3,2,1,0:T(8,128)(2,1)} %bitcast.7, bf16[4,4,48,256]{3,2,1,0:T(8,128)(2,1)} %bitcast.8, bf16[3,768,256]{2,1,0:T(8,128)(2,1)} %bitcast.6, ...), custom_call_target="tpu_custom_call" | custom-call | tf_op jit(solution)/shard_map/pallas_call | solution.py:496
  41.4 2.5 %shard_map.76 = (bf16[4,4,48,256]{3,2,1,0:T(8,128)(2,1)}, bf16[4,4,48,256]{3,2,1,0:T(8,128)(2,1)}, bf16[9,256,256]{2,1,0:T(8,128)(2,1)}, bf16[3,256,256]{2,1,0:T(8,128)(2,1)}) custom-call(bf16[4,4,48,256]{3,2,1,0:T(8,128)(2,1)} %get-tuple-element.12.refs_0_, bf16[4,4,48,256]{3,2,1,0:T(8,128)(2,1)} %get-tuple-element.13.refs_1_, ...), custom_call_target="tpu_custom_call" | custom-call | tf_op jit(solution)/shard_map/pallas_call | solution.py:536

commit v6 on v5

--- a/solution.py
+++ b/solution.py
@@ -72,7 +72,7 @@
     sizes, scale,
     x_hbm, c_hbm, ws_hbm, wt_hbm,
     dec_hbm, ig_hbm, sg_hbm, tg_hbm,
-    dec_ref, ig_ref,    x_ref, c_ref, ws_ref, wt_ref, xh, ch, soh, fgh, so, fg, s_buf, t_buf, acc, sb, rb, full,
+    dec_ref, ig_ref,    x_ref, c_ref, ws_ref, wt_ref, xh, ch, soh, fgh, so, fg, s_buf, t_buf, acc, sb, rb, full, turned, so_t, fg_t,
     load_sem, store_sem, halo_send, halo_recv, sum_send, sum_recv,
 ):
     frames, rows, cols, chan = x_ref.shape
@@ -193,12 +193,12 @@
                 acc[g, t * chan : (t + 1) * chan] += extra * scale
 
     def temporal_term(tap):
-        put_term(tap, dot_tn(so[...].reshape(cells, chan), later(2 - (tap - 9))))
+        put_term(tap, dot_nn(so_t[...], later(2 - (tap - 9))))
 
     def spatial_term(tap):
         i, j = tap // 3, tap % 3
         left = s_buf[:, i : i + rows, :, j * chan : (j + 1) * chan].reshape(cells, chan)
-        put_term(tap, dot_tn(left, fg[...].reshape(cells, chan)))
+        put_term(tap, dot_nn(fg_t[...], left))
 
     def later(offset):
         if offset == 0:
@@ -206,6 +206,7 @@
         parts = [c_ref[offset:], ch[:offset]]
         return jnp.concatenate(parts, axis=0).reshape(cells, chan)
 
+    so_t[...] = so[...].reshape(cells, chan).T
     temporal_term(11)
 
     @pl.when(has_next)
@@ -329,6 +330,7 @@
         fg[0] = (fg_sum[: rows * cols] + fold).astype(BF16).reshape(rows, cols, chan)
 
     pl.when(has_up)(fg_up.start)
+    fg_t[...] = fg[...].reshape(cells, chan).T
     pl.when(has_down)(fg_down.start)
 
     store_dec = pltpu.make_async_copy(dec_ref, dec_hbm, store_sem.at[0])
@@ -337,9 +339,8 @@
     def store_tap(tap):
         g, t = tap // per_group, tap % per_group
         to = sg_hbm.at[tap] if tap < 9 else tg_hbm.at[tap - 9]
-        return pltpu.make_async_copy(
-            full.at[g, t * chan : (t + 1) * chan], to, store_sem.at[2 + tap]
-        )
+        source = turned.at[tap] if tap < 9 else full.at[g, t * chan : (t + 1) * chan]
+        return pltpu.make_async_copy(source, to, store_sem.at[2 + tap])
 
     def make_decoded(start, count):
         def earlier(back):
@@ -420,7 +421,10 @@
         gather_copies(g, 1)[1].wait_recv()
         copies[0].wait_recv()
         for t in range(per_group):
-            store_tap(per_group * g + t).start()
+            tap = per_group * g + t
+            if tap < 9:
+                turned[tap] = full[g, t * chan : (t + 1) * chan].T
+            store_tap(tap).start()
 
     def terms(g):
         for tap in range(per_group * g, per_group * g + per_group):
@@ -522,6 +526,9 @@
             pltpu.VMEM((GROUPS, buffer_rows, chan), BF16),
             pltpu.VMEM((GROUPS, buffer_rows, chan), BF16),
             pltpu.VMEM((GROUPS, group_rows, chan), BF16),
+            pltpu.VMEM((9, chan, chan), BF16),
+            pltpu.VMEM((chan, frames * rows * cols), BF16),
+            pltpu.VMEM((chan, frames * rows * cols), BF16),
             pltpu.SemaphoreType.DMA((4,)),
             pltpu.SemaphoreType.DMA((14,)),
             pltpu.SemaphoreType.DMA((6,)),

time: 44.1 us -> 44.2 us (level)
  no operation moved by 1% of the time
where the time goes in v6:
time: 44.2 us; the launch traced here: 44.1 us
  Pallas kernels  43.4 us (98%)
  between operations  0.64 us (1%)
    pallas_call x1, Pallas kernels, local(): pl.pallas_call(functools.partial(kernel, sizes, 1.0 / math.sqrt(cell_coun...  40.9 us
    pallas_call x1, Pallas kernels, local(): pl.pallas_call(write_out, out_shape=tuple((jax.ShapeDtypeStruct(r.shape,...  2.49 us

profile of v6, /device:TPU:1, one launch (start us, length us, event | category | flops | bytes accessed | tf_op | source)
XLA Modules:
  0.0 44.1 jit_solution(5593654143822955032)
XLA Ops:
  0.6 40.9 %shard_map.75 = (bf16[4,4,48,256]{3,2,1,0:T(8,128)(2,1)}, bf16[4,4,48,256]{3,2,1,0:T(8,128)(2,1)}, bf16[9,256,256]{2,1,0:T(8,128)(2,1)}, bf16[3,256,256]{2,1,0:T(8,128)(2,1)}) custom-call(bf16[4,4,48,256]{3,2,1,0:T(8,128)(2,1)} %bitcast.7, bf16[4,4,48,256]{3,2,1,0:T(8,128)(2,1)} %bitcast.8, bf16[3,768,256]{2,1,0:T(8,128)(2,1)} %bitcast.6, ...), custom_call_target="tpu_custom_call" | custom-call | tf_op jit(solution)/shard_map/pallas_call | solution.py:500
  41.6 2.5 %shard_map.76 = (bf16[4,4,48,256]{3,2,1,0:T(8,128)(2,1)}, bf16[4,4,48,256]{3,2,1,0:T(8,128)(2,1)}, bf16[9,256,256]{2,1,0:T(8,128)(2,1)}, bf16[3,256,256]{2,1,0:T(8,128)(2,1)}) custom-call(bf16[4,4,48,256]{3,2,1,0:T(8,128)(2,1)} %get-tuple-element.12.refs_0_, bf16[4,4,48,256]{3,2,1,0:T(8,128)(2,1)} %get-tuple-element.13.refs_1_, ...), custom_call_target="tpu_custom_call" | custom-call | tf_op jit(solution)/shard_map/pallas_call | solution.py:543

commit v7 on v6

--- a/solution.py
+++ b/solution.py
@@ -216,8 +216,6 @@
     @pl.when(jnp.logical_not(has_next))
     def _():
         ch[...] = jnp.zeros(ch.shape, BF16)
-
-    pl.when(has_next)(so_next.start)
 
     def sum_copy(g, at, size, slot, flips):
         place = (g, pl.ds(at, size))
@@ -329,9 +327,7 @@
         fold = dot_nt(c0, wt_ref[0]) + dot_nt(c0, wt_ref[1]) + dot_nt(c1, wt_ref[0])
         fg[0] = (fg_sum[: rows * cols] + fold).astype(BF16).reshape(rows, cols, chan)
 
-    pl.when(has_up)(fg_up.start)
     fg_t[...] = fg[...].reshape(cells, chan).T
-    pl.when(has_down)(fg_down.start)
 
     store_dec = pltpu.make_async_copy(dec_ref, dec_hbm, store_sem.at[0])
     store_ig = pltpu.make_async_copy(ig_ref, ig_hbm, store_sem.at[1])
@@ -441,10 +437,19 @@
         for level in range(3):
             after = 8 + 4 * (steps - 3) + 3 * (level + 1)
             events.append((n + after + 0.2, functools.partial(gather, g, level)))
-    units = [decoded_later, grad_taps_inner, decoded_earlier, grad_taps_outer]
-    units += [functools.partial(make_input_grad, f, 1) for f in range(frames)] + [store_ig.start]
-    for n, unit in enumerate(units):
-        events.append((GROUPS + 0.5 + n, unit))
+    def send_frame_grad():
+        pl.when(has_up)(fg_up.start)
+        pl.when(has_down)(fg_down.start)
+
+    def send_spatial_out():
+        pl.when(has_next)(so_next.start)
+
+    events += [
+        (5.6, send_frame_grad), (6.5, decoded_later), (7.7, send_spatial_out),
+        (8.5, grad_taps_inner), (11.5, grad_taps_outer), (17.5, decoded_earlier),
+    ]
+    events += [(12.5 + f, functools.partial(make_input_grad, f, 1)) for f in range(frames)]
+    events.append((12.5 + frames, store_ig.start))
     for _, event in sorted(events, key=lambda e: e[0]):
         event()
 

time: 44.2 us -> 46.8 us (1.059)
  Pallas kernels: 43.4 us -> 46 us
    pallas_call x1, Pallas kernels: 40.9 us -> 43.5 us  [local(): pl.pallas_call(functools.partial(kernel, sizes, 1.0 / math.sqrt(cell_coun...]
where the time goes in v7:
time: 46.8 us; the launch traced here: 46.7 us
  Pallas kernels  46 us (98%)
  between operations  0.64 us (1%)
    pallas_call x1, Pallas kernels, local(): pl.pallas_call(functools.partial(kernel, sizes, 1.0 / math.sqrt(cell_coun...  43.5 us
    pallas_call x1, Pallas kernels, local(): pl.pallas_call(write_out, out_shape=tuple((jax.ShapeDtypeStruct(r.shape,...  2.49 us

profile of v7, /device:TPU:1, one launch (start us, length us, event | category | flops | bytes accessed | tf_op | source)
XLA Modules:
  0.0 46.7 jit_solution(16358074063508813635)
XLA Ops:
  0.6 43.5 %shard_map.75 = (bf16[4,4,48,256]{3,2,1,0:T(8,128)(2,1)}, bf16[4,4,48,256]{3,2,1,0:T(8,128)(2,1)}, bf16[9,256,256]{2,1,0:T(8,128)(2,1)}, bf16[3,256,256]{2,1,0:T(8,128)(2,1)}) custom-call(bf16[4,4,48,256]{3,2,1,0:T(8,128)(2,1)} %bitcast.7, bf16[4,4,48,256]{3,2,1,0:T(8,128)(2,1)} %bitcast.8, bf16[3,768,256]{2,1,0:T(8,128)(2,1)} %bitcast.6, ...), custom_call_target="tpu_custom_call" | custom-call | tf_op jit(solution)/shard_map/pallas_call | solution.py:505
  44.2 2.5 %shard_map.76 = (bf16[4,4,48,256]{3,2,1,0:T(8,128)(2,1)}, bf16[4,4,48,256]{3,2,1,0:T(8,128)(2,1)}, bf16[9,256,256]{2,1,0:T(8,128)(2,1)}, bf16[3,256,256]{2,1,0:T(8,128)(2,1)}) custom-call(bf16[4,4,48,256]{3,2,1,0:T(8,128)(2,1)} %get-tuple-element.12.refs_0_, bf16[4,4,48,256]{3,2,1,0:T(8,128)(2,1)} %get-tuple-element.13.refs_1_, ...), custom_call_target="tpu_custom_call" | custom-call | tf_op jit(solution)/shard_map/pallas_call | solution.py:548
